TPU v7x, 256 devices: a whole 4x4x8 slice. The times are simulated.
256 devices in a mesh: stn: 64 (over y_hi, z, x), grp: 4 (over y_lo, core).
Axes of the slice: x: 4, y: 4 (y_hi: 2, y_lo: 2; y = y_hi * 2 + y_lo), z: 8, core: 2. Of those that a mesh axis runs over, the one named last changes fastest.
Arguments:
- voltages: bfloat16 [2, 128, 2, 180224], P(None, 'stn', None, 'grp'), may hold values from -6 to 6
- corr_taps: float32 [12, 4096], replicated, may hold values from -1.75 to 1.75
- beam_taps: float32 [12, 256], replicated, may hold values from -1.75 to 1.75
- angle_table: float32 [64, 256], replicated, may hold values from -3.140625 to 3.140625
- table_index: int32 [16, 128], replicated, may hold values from 0 to 63
Outputs:
- visibility: float32 [64, 256, 2, 256], P('stn', 'grp')
- beam_power: float32 [256, 16, 704], P('stn', None, 'grp')
All inputs are finite; a program needn't handle non-finite values.
Results may differ from a plain program's by a relative error of at most 0.0046.
Values may be sent and summed in bfloat16 or wider, within the bound.
A program may use at most 128 MiB of HBM per device.

v0:
```python
import math

import jax
import jax.numpy as jnp
from jax import lax
from jax.sharding import PartitionSpec as P

RADIX = 64


def from_behind(array, axis, by):
    devices = lax.axis_size(axis)
    pairs = [(i, i + by) for i in range(devices) if 0 <= i + by < devices]
    return lax.ppermute(array, axis, pairs)


def dft_tables(length):
    positions = jnp.arange(length, dtype=jnp.int32)
    phases = (positions[:, None] * positions[None, :] % length).astype(jnp.float32) * (
        2.0 * math.pi / length
    )
    factor = 1.0 / math.sqrt(length)
    return (
        (jnp.cos(phases) * factor).astype(jnp.bfloat16),
        (jnp.sin(phases) * factor).astype(jnp.bfloat16),
    )


def twiddles(radix_size):
    positions = jnp.arange(radix_size, dtype=jnp.int32)
    whole = radix_size * radix_size
    phases = (positions[:, None] * positions[None, :] % whole).astype(jnp.float32) * (
        2.0 * math.pi / whole
    )
    return (jnp.cos(phases), jnp.sin(phases))


def polyphase(extended, coefficients, frame_count):
    tap_count, length = coefficients.shape
    shaped = extended.reshape(extended.shape[:-1] + (frame_count + tap_count - 1, length))
    summed = jnp.zeros(shaped.shape[:-2] + (frame_count, length), jnp.float32)
    for tap_index in range(tap_count):
        lead_frame = tap_count - 1 - tap_index
        summed = (
            summed
            + shaped[..., lead_frame : lead_frame + frame_count, :].astype(jnp.float32)
            * coefficients[tap_index]
        )
    return summed.astype(jnp.bfloat16)


def contract(pattern, left_side, right_side):
    return jnp.einsum(pattern, left_side, right_side, preferred_element_type=jnp.float32)


def long_transform(real_part, imag_part):
    cos_table, sin_table = dft_tables(RADIX)
    twist_cos, twist_sin = twiddles(RADIX)
    split_shape = real_part.shape[:-1] + (RADIX, RADIX)
    real_part = real_part.reshape(split_shape)
    imag_part = imag_part.reshape(split_shape)
    first_form = "...ab,ak->...kb"
    middle_real = contract(first_form, real_part, cos_table) + contract(
        first_form, imag_part, sin_table
    )
    middle_imag = contract(first_form, imag_part, cos_table) - contract(
        first_form, real_part, sin_table
    )
    twisted_real = (middle_real * twist_cos + middle_imag * twist_sin).astype(jnp.bfloat16)
    twisted_imag = (middle_imag * twist_cos - middle_real * twist_sin).astype(jnp.bfloat16)
    second_form = "...kb,bm->...mk"
    result_real = contract(second_form, twisted_real, cos_table) + contract(
        second_form, twisted_imag, sin_table
    )
    result_imag = contract(second_form, twisted_imag, cos_table) - contract(
        second_form, twisted_real, sin_table
    )
    flat_shape = split_shape[:-2] + (RADIX * RADIX,)
    return jnp.stack(
        [
            result_real.astype(jnp.bfloat16).reshape(flat_shape),
            result_imag.astype(jnp.bfloat16).reshape(flat_shape),
        ],
        0,
    )


def short_transform(real_part, imag_part):
    cos_table, sin_table = dft_tables(real_part.shape[-1])
    pattern = "...n,nk->...k"
    result_real = contract(pattern, real_part, cos_table) + contract(pattern, imag_part, sin_table)
    result_imag = contract(pattern, imag_part, cos_table) - contract(pattern, real_part, sin_table)
    return jnp.stack([result_real.astype(jnp.bfloat16), result_imag.astype(jnp.bfloat16)], 0)


def station_weights(index_rows, columns, station_total):
    table_rows = jnp.arange(columns.shape[0], dtype=jnp.int32)
    one_hot = (index_rows[..., None] == table_rows).astype(jnp.float32)
    angles = jnp.einsum("bst,tc->bsc", one_hot, columns, precision=lax.Precision.HIGHEST)
    factor = 1.0 / math.sqrt(station_total)
    return (
        (jnp.cos(angles) * factor).astype(jnp.bfloat16),
        (jnp.sin(angles) * factor).astype(jnp.bfloat16),
    )


def beam_terms(weight_real, weight_imag, spec_real, spec_imag):
    pattern = "bsc,sptc->cpbt"
    real_part = contract(pattern, weight_real, spec_real) - contract(
        pattern, weight_imag, spec_imag
    )
    imag_part = contract(pattern, weight_real, spec_imag) + contract(
        pattern, weight_imag, spec_real
    )
    return jnp.stack([real_part, imag_part], 1)


def on_device(voltages, corr_taps, beam_taps, angle_table, table_index):
    tap_count = corr_taps.shape[0]
    length = corr_taps.shape[1]
    short_length = beam_taps.shape[1]
    local_stations = voltages.shape[1]
    samples = voltages.shape[3]
    station_total = local_stations * lax.axis_size("stn")
    history = from_behind(voltages, "grp", 1)
    extended = jnp.concatenate([history, voltages], 3)
    filtered = polyphase(extended, corr_taps, samples // length)
    spectra = long_transform(filtered[0], filtered[1])
    short_input = extended[..., (tap_count - 1) * (length - short_length) :]
    short_filtered = polyphase(short_input, beam_taps, samples // short_length)
    short_spectra = short_transform(short_filtered[0], short_filtered[1])
    turned = lax.all_to_all(spectra, "stn", split_axis=4, concat_axis=1, tiled=True)
    own_rows = lax.dynamic_slice_in_dim(
        table_index, lax.axis_index("stn") * local_stations, local_stations, 1
    )
    weight_real, weight_imag = station_weights(own_rows, angle_table, station_total)
    beam_fields = lax.psum_scatter(
        beam_terms(weight_real, weight_imag, short_spectra[0], short_spectra[1]),
        "stn",
        scatter_dimension=0,
        tiled=True,
    )
    beam_power = jnp.sum(beam_fields[:, 0] ** 2 + beam_fields[:, 1] ** 2, axis=1)
    signals = turned.shape[1] * turned.shape[2]
    inner_depth = turned.shape[3] * turned.shape[4]
    flat_real = turned[0].reshape(signals, inner_depth)
    flat_imag = turned[1].reshape(signals, inner_depth)
    stacked = jnp.concatenate([flat_real, flat_imag], 1)
    rotated = jnp.concatenate([flat_imag, -flat_real], 1)
    real_part = lax.dot_general(
        stacked, stacked, (((1,), (1,)), ((), ())), preferred_element_type=jnp.float32
    )
    imag_part = lax.dot_general(
        rotated, stacked, (((1,), (1,)), ((), ())), preferred_element_type=jnp.float32
    )
    summed = lax.psum_scatter(
        jnp.stack([real_part, imag_part], 1), "grp", scatter_dimension=0, tiled=True
    )
    visibility = (summed * (1.0 / math.sqrt(inner_depth * lax.axis_size("grp"))))[None]
    return (visibility, beam_power)


def solution(mesh):
    in_specs = (P(None, "stn", None, "grp"), P(), P(), P(), P())
    out_specs = (P("stn", "grp", None, None), P("stn", None, "grp"))
    return jax.shard_map(
        on_device, mesh=mesh, in_specs=in_specs, out_specs=out_specs, check_vma=False
    )
```

profile of v0, /device:TPU:2, one launch (start us, length us, event | category | flops | bytes accessed | tf_op | source)
XLA Modules:
  0.0 938.9 jit_solution(10486835199044593990)
XLA Ops:
  8.0 1.9 collective-permute-start
  14.2 2.0 fusion.123
  18.2 1.4 slice.246
  19.6 1.5 reshape.79
  21.1 2.3 add_convert_fusion.1
  23.4 2.1 fusion.12
  25.5 2.1 fusion.11
  27.6 3.4 add_convert_fusion
  42.0 14.6 %copy.75 = bf16[2,2,2,11,4096]{3,2,1,0,4:T(2,128)(2,1)} copy(bf16[2,2,2,11,4096]{4,2,3,1,0:T(2,128)(2,1)S(1)} %pad_maximum_fusion.1) | data formatting | bytes 1441792 | tf_op jit(solution)/shard_map/stack | solution.py:79
  56.6 14.0 %reshape.96 = bf16[64,2,2816]{2,1,0:T(2,128)(2,1)} reshape(bf16[4096,2,2,2,11]{4,3,2,1,0:T(2,128)(2,1)} %bitcast.124) | data formatting | bytes 1441792
  70.5 14.8 %all-to-all-start = ((bf16[64,2,2816]{2,1,0:T(2,128)(2,1)}), bf16[64,2,2816]{2,1,0:T(2,128)(2,1)S(1)}, u32[]{:S(2)}, u32[]{:S(2)}) async-start(bf16[64,2,2816]{2,1,0:T(2,128)(2,1)} %reshape.96), calls=%async_computation | async-start | bytes 1441792 | tf_op jit(solution)/shard_map/all_to_all | solution.py:132
  85.6 2.3 fusion.5
  87.9 1.2 fusion.4
  90.1 1.3 fusion.130
  91.4 4.5 fusion.129
  96.0 4.6 add_bitcast_fusion
  100.6 5.0 all-to-all-done
  105.5 19.3 %reshape.97 = bf16[4096,2,2,2,11]{4,3,2,1,0:T(2,128)(2,1)} reshape(bf16[64,2,2816]{2,1,0:T(2,128)(2,1)S(1)} %all-to-all-done) | data formatting | bytes 1441792
  124.9 19.8 %copy.99 = bf16[2,2,2,11,64,64]{5,4,2,3,1,0:T(8,128)(2,1)S(1)} copy(bf16[2,2,2,11,64,64]{3,2,1,0,5,4:T(2,128)(2,1)} %bitcast.125) | data formatting | bytes 1441792 | tf_op jit(solution)/shard_map/all_to_all | solution.py:132
  149.1 4.7 subtract_bitcast_fusion
  153.8 10.3 %pad_maximum_fusion = f32[256,2,2,16,176]{4,3,2,0,1:T(8,128)} fusion(f32[256,1,2,16,176]{4,3,2,0,1:T(8,128)} %add_bitcast_fusion, f32[256,1,2,16,176]{4,3,2,0,1:T(8,128)S(1)} %subtract_bitcast_fusion), kind=kLoop, calls=%fused_computation | loop fusion | flops 2883584 | bytes 23068672 | tf_op jit(solution)/shard_map/stack | solution.py:115
  166.0 4.3 reduce-scatter.3.cloned.1.call-done
  172.0 757.9 %all-reduce.3.cloned.1.call-done = f32[256,2,2,16,176]{4,3,2,0,1:T(8,128)} async-done(((f32[256,2,2,16,176]{4,3,2,0,1:T(8,128)}), f32[256,2,2,16,176]{4,3,2,0,1:T(8,128)}) %all-reduce.3.cloned.1.call-update) | async-done | bytes 11534352
  929.9 1.6 fusion.22
  (68 shorter events, 25.6 us)
Async XLA Ops:
  8.0 4.3 copy-start
  8.0 8.7 copy-start.5
  8.0 8.2 collective-permute-start
  23.4 4.1 copy-start.6
  39.9 1.1 copy-start.2
  70.5 15.1 %copy-start.7 = (bf16[2,2,2,176,256]{4,3,2,1,0:T(8,128)(2,1)S(1)}, bf16[2,2,2,176,256]{4,3,2,1,0:T(8,128)(2,1)}, u32[]{:S(2)}) copy-start(bf16[2,2,2,176,256]{4,3,2,1,0:T(8,128)(2,1)} %copy-done.6) | copy-start | bytes 2162692
  70.5 17.4 %copy-start.9 = (f32[2,2,176,256]{3,2,1,0:T(8,128)S(1)}, f32[2,2,176,256]{3,2,1,0:T(8,128)}, u32[]{:S(2)}) copy-start(f32[2,2,176,256]{3,2,1,0:T(8,128)} %fusion.11) | copy-start | bytes 2162692
  70.5 35.0 %all-to-all-start = ((bf16[64,2,2816]{2,1,0:T(2,128)(2,1)}), bf16[64,2,2816]{2,1,0:T(2,128)(2,1)S(1)}, u32[]{:S(2)}, u32[]{:S(2)}) async-start(bf16[64,2,2816]{2,1,0:T(2,128)(2,1)} %reshape.96), calls=%async_computation | async-start | bytes 1441792 | tf_op jit(solution)/shard_map/all_to_all | solution.py:132
  85.3 85.0 %reduce-scatter.3.cloned.1.call-start = ((), (), s32[]{:S(2)}) async-start(), calls=%async_computation.2 | async-start | bytes 655360 | tf_op jit(solution)/shard_map/reduce_scatter | solution.py:156
  87.9 2.2 copy-start.4
  91.4 4.6 copy-start.3
  149.0 780.9 %all-reduce.3.cloned.1.call-start = ((), (), s32[]{:S(2)}) async-start(), calls=%async_computation.3 | async-start | bytes 33554432
  164.1 0.7 copy-start.8
  164.1 767.4 %copy-start.1 = (f32[64,256]{1,0:T(8,128)S(1)}, f32[64,256]{1,0:T(8,128)}, u32[]{:S(2)}) copy-start(f32[64,256]{1,0:T(8,128)} %param.8) | copy-start | bytes 196612
Sparse Core Ops, SparseCore 0:
  149.1 21.1 reduce-scatter.2
Sparse Core Ops, SparseCore 1:
  164.2 765.6 all-reduce.2
where the time goes:
time: 940 us; the launch traced here: 939 us
  waiting for transfers between devices  767 us (82%)
  local copies, waits for them, and re-layouts  87.9 us (9%)
  matrix products  29.6 us (3%)
  other arithmetic  20.8 us (2%)
  starting transfers between devices  17 us (2%)
  between operations  16.5 us (2%)
    unnamed x3, waiting for transfers between devices  758 us
    unnamed x25, local copies, waits for them, and re-layouts  35.8 us
    dot_general x16, matrix products, contract(): jnp.einsum(pattern, left_side, right_side, preferred_element_type=jnp.flo...  28.3 us
    all_to_all x1, local copies, waits for them, and re-layouts, on_device(): lax.all_to_all(spectra, 'stn', split_axis=4, concat_axis=1, tiled=True)  19.8 us
  transfers between devices with their start and end apart: 4, of which 3 were waited for; matrix products, arithmetic and copies ran while one was open for 4% of the time, Pallas kernels for 0%

commit v1 on v0

--- a/solution.py
+++ b/solution.py
@@ -104,17 +104,6 @@
     )
 
 
-def beam_terms(weight_real, weight_imag, spec_real, spec_imag):
-    pattern = "bsc,sptc->cpbt"
-    real_part = contract(pattern, weight_real, spec_real) - contract(
-        pattern, weight_imag, spec_imag
-    )
-    imag_part = contract(pattern, weight_real, spec_imag) + contract(
-        pattern, weight_imag, spec_real
-    )
-    return jnp.stack([real_part, imag_part], 1)
-
-
 def on_device(voltages, corr_taps, beam_taps, angle_table, table_index):
     tap_count = corr_taps.shape[0]
     length = corr_taps.shape[1]
@@ -130,17 +119,23 @@
     short_filtered = polyphase(short_input, beam_taps, samples // short_length)
     short_spectra = short_transform(short_filtered[0], short_filtered[1])
     turned = lax.all_to_all(spectra, "stn", split_axis=4, concat_axis=1, tiled=True)
-    own_rows = lax.dynamic_slice_in_dim(
-        table_index, lax.axis_index("stn") * local_stations, local_stations, 1
+    moved = lax.all_to_all(
+        short_spectra.transpose(4, 0, 1, 2, 3), "stn", split_axis=0, concat_axis=2, tiled=True
     )
-    weight_real, weight_imag = station_weights(own_rows, angle_table, station_total)
-    beam_fields = lax.psum_scatter(
-        beam_terms(weight_real, weight_imag, short_spectra[0], short_spectra[1]),
-        "stn",
-        scatter_dimension=0,
-        tiled=True,
+    own_channels = short_length // lax.axis_size("stn")
+    own_columns = lax.dynamic_slice_in_dim(
+        angle_table, lax.axis_index("stn") * own_channels, own_channels, 1
     )
-    beam_power = jnp.sum(beam_fields[:, 0] ** 2 + beam_fields[:, 1] ** 2, axis=1)
+    weight_real, weight_imag = station_weights(table_index, own_columns, station_total)
+    spec_real, spec_imag = moved[:, 0], moved[:, 1]
+    pattern = "bsc,cspt->cpbt"
+    beam_real = contract(pattern, weight_real, spec_real) - contract(
+        pattern, weight_imag, spec_imag
+    )
+    beam_imag = contract(pattern, weight_real, spec_imag) + contract(
+        pattern, weight_imag, spec_real
+    )
+    beam_power = jnp.sum(beam_real**2 + beam_imag**2, axis=1)
     signals = turned.shape[1] * turned.shape[2]
     inner_depth = turned.shape[3] * turned.shape[4]
     flat_real = turned[0].reshape(signals, inner_depth)

time: 940 us -> 197 us (0.21)
  the two profiles are of different devices: /device:TPU:2 before, /device:TPU:1 now
where the time goes in v1:
time: 197 us; the launch traced here: 196 us
  local copies, waits for them, and re-layouts  91.7 us (47%)
  waiting for transfers between devices  32.6 us (17%)
  starting transfers between devices  31.5 us (16%)
  matrix products  16.5 us (8%)
  between operations  14.5 us (7%)
  other arithmetic  8.7 us (4%)
    unnamed x34, local copies, waits for them, and re-layouts  36 us
    all_to_all x1, local copies, waits for them, and re-layouts, on_device(): lax.all_to_all(spectra, 'stn', split_axis=4, concat_axis=1, tiled=True)  19.8 us
    another operation x5, local copies, waits for them, and re-layouts, long_transform(): jnp.stack([result_real.astype(jnp.bfloat16).reshape(flat_shape), result_i...  19.1 us
    all_to_all x1, waiting for transfers between devices, on_device(): lax.all_to_all(spectra, 'stn', split_axis=4, concat_axis=1, tiled=True)  16.8 us
    dot_general x16, matrix products, contract(): jnp.einsum(pattern, left_side, right_side, preferred_element_type=jnp.flo...  15.1 us
    all_to_all x1, starting transfers between devices, on_device(): lax.all_to_all(short_spectra.transpose(4, 0, 1, 2, 3), 'stn', split_axis=...  14.2 us
    all_to_all x1, starting transfers between devices, on_device(): lax.all_to_all(spectra, 'stn', split_axis=4, concat_axis=1, tiled=True)  12.4 us
    reduce_scatter x1, waiting for transfers between devices, on_device(): lax.psum_scatter(jnp.stack([real_part, imag_part], 1), 'grp', scatter_dim...  11.2 us
  transfers between devices with their start and end apart: 4, of which 3 were waited for; matrix products, arithmetic and copies ran while one was open for 25% of the time, Pallas kernels for 0%

profile of v1, /device:TPU:1, one launch (start us, length us, event | category | flops | bytes accessed | tf_op | source)
XLA Modules:
  0.0 195.6 jit_solution(5770129710685628864)
XLA Ops:
  7.2 4.7 %collective-permute-start = (bf16[2,2,2,45056]{3,2,1,0:T(2,128)(2,1)}, bf16[2,2,2,45056]{3,2,1,0:T(2,128)(2,1)S(1)}, u32[]{:S(2)}, u32[]{:S(2)}) collective-permute-start(bf16[2,2,2,45056]{3,2,1,0:T(2,128)(2,1)} %param.5), channel_id=1, source_target_pairs={{0,1},{1,2},{2,3},{4,5},{5,6},{6,7},{8,9},{9,10},{10,11},{12,13},{... | collective-permute-start | bytes 2162696 | tf_op jit(solution)/shard_map/ppermute | solution.py:14
  12.2 1.6 fusion.145
  14.0 1.9 fusion.144
  15.9 4.5 %collective-permute-done = bf16[2,2,2,45056]{3,2,1,0:T(2,128)(2,1)S(1)} collective-permute-done((bf16[2,2,2,45056]{3,2,1,0:T(2,128)(2,1)}, bf16[2,2,2,45056]{3,2,1,0:T(2,128)(2,1)S(1)}, u32[]{:S(2)}, u32[]{:S(2)}) %collective-permute-start) | collective-permute-done | bytes 720928 | tf_op jit(solution)/shard_map/ppermute | solution.py:14
  21.5 1.4 slice.246
  23.9 1.5 reshape.76
  25.5 2.3 %add_convert_fusion.1 = bf16[2,2,2,176,256]{4,3,2,1,0:T(8,128)(2,1)S(1)} fusion(bf16[2,2,2,187,256]{4,3,2,1,0:T(8,128)(2,1)S(1)} %reshape.76, f32[256]{0:T(256)S(1)} %bitcast.157, f32[256]{0:T(256)S(1)} %bitcast.158, f32[256]{0:T(256)S(1)} %bitcast.148, f32[256]{0:T(256)S(1)} %bitcast.149, f32[256]{0:T(256)S(1)} %bitcast.150, f32[256]{0:T(256)S(1)} %bitcast.151, ...), kind=kLoop, calls=%fused_computation.5 | loop fusion | flops 12976128 | bytes 9383936 | tf_op jit(solution)/shard_map/convert_element_type | solution.py:49
  27.8 2.1 %fusion.25 = f32[2,2,176,256]{3,2,1,0:T(8,128)} fusion(bf16[2,2,2,176,256]{4,3,2,1,0:T(8,128)(2,1)S(1)} %add_convert_fusion.1), kind=kOutput, calls=%fused_computation.49 | convolution fusion | flops 93323264 | bytes 1081344 | tf_op jit(solution)/shard_map/...n,nk->...k/dot_general | solution.py:53
  29.9 2.1 %fusion.24 = f32[2,2,176,256]{3,2,1,0:T(8,128)} fusion(bf16[2,2,2,176,256]{4,3,2,1,0:T(8,128)(2,1)S(1)} %add_convert_fusion.1), kind=kOutput, calls=%fused_computation.48 | convolution fusion | flops 93323264 | bytes 1081344 | tf_op jit(solution)/shard_map/...n,nk->...k/dot_general | solution.py:53
  32.0 3.2 %add_convert_fusion = bf16[2,2,2,11,4096]{4,3,2,1,0:T(8,128)(2,1)S(1)} fusion(bf16[2,2,2,22,4096]{4,3,2,1,0:T(8,128)(2,1)S(1)} %reshape.75, f32[4096]{0:T(1024)S(1)} %bitcast.144, f32[4096]{0:T(1024)S(1)} %bitcast.145, f32[4096]{0:T(1024)S(1)} %bitcast.135, f32[4096]{0:T(1024)S(1)} %bitcast.136, f32[4096]{0:T(1024)S(1)} %bitcast.137, f32[4096]{0:T(1024)S(1)} %bitcast.138, ...), kind=kLoop, calls=%fused_computation | loop fusion | flops 12976128 | bytes 9568256 | tf_op jit(solution)/shard_map/convert_element_type | solution.py:49
  36.8 2.4 %fusion.6 = bf16[1,2,2,176,256]{4,3,2,1,0:T(8,128)(2,1)S(1)} fusion(f32[2,2,176,256]{3,2,1,0:T(8,128)} %fusion.25, bf16[2,2,2,176,256]{4,3,2,1,0:T(8,128)(2,1)S(1)} %add_convert_fusion.1), kind=kOutput, calls=%fused_computation.16 | convolution fusion | flops 93683712 | bytes 1441792 | tf_op jit(solution)/shard_map/...n,nk->...k/dot_general | solution.py:53
  39.2 1.2 fusion.7
  40.5 2.1 %copy.100 = bf16[256,2,2,2,176]{4,3,2,1,0:T(2,128)(2,1)} copy(bf16[256,2,2,2,176]{0,4,3,2,1:T(8,128)(2,1)S(1)} %maximum_bitcast_fusion) | data formatting | bytes 1441792 | tf_op jit(solution)/shard_map/transpose | solution.py:123
  42.7 14.2 %all-to-all-start.1 = ((bf16[256,2,2,2,176]{4,3,2,1,0:T(2,128)(2,1)}), bf16[256,2,2,2,176]{4,3,2,1,0:T(2,128)(2,1)S(1)}, u32[]{:S(2)}, u32[]{:S(2)}) async-start(bf16[256,2,2,2,176]{4,3,2,1,0:T(2,128)(2,1)} %copy.100), calls=%async_computation.2 | async-start | bytes 2097152 | tf_op jit(solution)/shard_map/all_to_all | solution.py:122
  60.6 1.5 reshape.84
  62.1 2.2 %copy.114 = bf16[1,2,2,11,4096]{4,2,3,1,0:T(2,128)(2,1)} copy(bf16[1,2,2,11,4096]{4,3,2,1,0:T(8,128)(2,1)} %reshape.84) | data formatting | bytes 720896 | tf_op jit(solution)/shard_map/stack;reshape | solution.py:79
  68.1 14.4 %copy.96 = bf16[2,2,2,11,4096]{3,2,1,0,4:T(2,128)(2,1)} copy(bf16[2,2,2,11,4096]{4,2,3,1,0:T(2,128)(2,1)S(1)} %pad_maximum_fusion) | data formatting | bytes 1441792 | tf_op jit(solution)/shard_map/stack | solution.py:79
  82.5 13.9 %reshape.88 = bf16[64,2,2816]{2,1,0:T(2,128)(2,1)} reshape(bf16[4096,2,2,2,11]{4,3,2,1,0:T(2,128)(2,1)} %bitcast.129) | data formatting | bytes 1441792
  96.5 12.4 %all-to-all-start = ((bf16[64,2,2816]{2,1,0:T(2,128)(2,1)}), bf16[64,2,2816]{2,1,0:T(2,128)(2,1)S(1)}, u32[]{:S(2)}, u32[]{:S(2)}) async-start(bf16[64,2,2816]{2,1,0:T(2,128)(2,1)} %reshape.88), calls=%async_computation | async-start | bytes 1441792 | tf_op jit(solution)/shard_map/all_to_all | solution.py:121
  109.5 1.9 copy.101
  111.4 16.8 %all-to-all-done = bf16[64,2,2816]{2,1,0:T(2,128)(2,1)S(1)} async-done(((bf16[64,2,2816]{2,1,0:T(2,128)(2,1)}), bf16[64,2,2816]{2,1,0:T(2,128)(2,1)S(1)}, u32[]{:S(2)}, u32[]{:S(2)}) %all-to-all-start) | async-done | bytes 720928 | tf_op jit(solution)/shard_map/all_to_all | solution.py:121
  128.2 19.4 %reshape.89 = bf16[4096,2,2,2,11]{4,3,2,1,0:T(2,128)(2,1)} reshape(bf16[64,2,2816]{2,1,0:T(2,128)(2,1)S(1)} %all-to-all-done) | data formatting | bytes 1441792
  147.7 19.8 %copy.116 = bf16[2,2,2,11,64,64]{5,4,2,3,1,0:T(8,128)(2,1)S(1)} copy(bf16[2,2,2,11,64,64]{3,2,1,0,5,4:T(2,128)(2,1)} %bitcast.130) | data formatting | bytes 1441792 | tf_op jit(solution)/shard_map/all_to_all | solution.py:121
  175.8 11.2 %reduce-scatter.2.cloned.1.call-done = f32[64,2,256]{2,0,1:T(8,128)} async-done(((f32[256,2,256]{2,0,1:T(8,128)}), f32[64,2,256]{2,0,1:T(8,128)}) %reduce-scatter.2.cloned.1.call-update) | async-done | bytes 131088 | tf_op jit(solution)/shard_map/reduce_scatter | solution.py:151
  (72 shorter events, 22.2 us)
Async XLA Ops:
  7.2 102.0 %copy-start = (f32[64,256]{1,0:T(8,128)S(1)}, f32[64,256]{1,0:T(8,128)}, u32[]{:S(2)}) copy-start(f32[64,256]{1,0:T(8,128)} %param.8) | copy-start | bytes 196612
  7.2 13.8 %copy-start.3 = (bf16[2,2,2,45056]{3,2,1,0:T(2,128)(2,1)S(1)}, bf16[2,2,2,45056]{3,2,1,0:T(2,128)(2,1)}, u32[]{:S(2)}) copy-start(bf16[2,2,2,45056]{3,2,1,0:T(2,128)(2,1)} %param.5) | copy-start | bytes 2162692
  7.2 13.3 %collective-permute-start = (bf16[2,2,2,45056]{3,2,1,0:T(2,128)(2,1)}, bf16[2,2,2,45056]{3,2,1,0:T(2,128)(2,1)S(1)}, u32[]{:S(2)}, u32[]{:S(2)}) collective-permute-start(bf16[2,2,2,45056]{3,2,1,0:T(2,128)(2,1)} %param.5), channel_id=1, source_target_pairs={{0,1},{1,2},{2,3},{4,5},{5,6},{6,7},{8,9},{9,10},{10,11},{12,13},{... | collective-permute-start | bytes 2162696 | tf_op jit(solution)/shard_map/ppermute | solution.py:14
  23.8 1.6 copy-start.4
  23.8 1.6 copy-start.5
  23.8 1.6 copy-start.6
  23.9 1.6 copy-start.7
  23.9 1.6 copy-start.8
  23.9 1.6 copy-start.9
  23.9 1.6 copy-start.10
  23.9 1.6 copy-start.11
  36.8 2.4 %copy-start.13 = (f32[2,2,176,256]{3,2,1,0:T(8,128)S(1)}, f32[2,2,176,256]{3,2,1,0:T(8,128)}, u32[]{:S(2)}) copy-start(f32[2,2,176,256]{3,2,1,0:T(8,128)} %fusion.24) | copy-start | bytes 2162692
  42.7 53.8 %all-to-all-start.1 = ((bf16[256,2,2,2,176]{4,3,2,1,0:T(2,128)(2,1)}), bf16[256,2,2,2,176]{4,3,2,1,0:T(2,128)(2,1)S(1)}, u32[]{:S(2)}, u32[]{:S(2)}) async-start(bf16[256,2,2,2,176]{4,3,2,1,0:T(2,128)(2,1)} %copy.100), calls=%async_computation.2 | async-start | bytes 2097152 | tf_op jit(solution)/shard_map/all_to_all | solution.py:122
  66.0 1.1 copy-start.2
  96.5 12.7 %copy-start.12 = (s32[16,128]{1,0:T(8,128)S(1)}, s32[16,128]{1,0:T(8,128)}, u32[]{:S(2)}) copy-start(s32[16,128]{1,0:T(8,128)} %param.9) | copy-start | bytes 24580
  96.5 31.7 %all-to-all-start = ((bf16[64,2,2816]{2,1,0:T(2,128)(2,1)}), bf16[64,2,2816]{2,1,0:T(2,128)(2,1)S(1)}, u32[]{:S(2)}, u32[]{:S(2)}) async-start(bf16[64,2,2816]{2,1,0:T(2,128)(2,1)} %reshape.88), calls=%async_computation | async-start | bytes 1441792 | tf_op jit(solution)/shard_map/all_to_all | solution.py:121
  108.9 78.2 %reduce-scatter.2.cloned.1.call-start = ((), (), s32[]{:S(2)}) async-start(), calls=%async_computation.3 | async-start | bytes 655360 | tf_op jit(solution)/shard_map/reduce_scatter | solution.py:151
  170.9 1.4 copy-start.1
Sparse Core Ops, SparseCore 0:
  171.9 15.0 reduce-scatter.1

commit v2 on v1

v2 whole, which is shorter than its diff:
```python
import functools
import math

import jax
import jax.numpy as jnp
import ml_dtypes
import numpy as np
from jax import lax
from jax.experimental import pallas as pl
from jax.experimental.pallas import tpu as pltpu
from jax.sharding import PartitionSpec as P

MESH = pl.DeviceIdType.MESH
BF = jnp.bfloat16
F32 = jnp.float32

RADIX = 64
TAPS = 12
STN = 64
GRP = 4
LANES = 128
TILES = 352
HALF = 176
FRAMES = 11
SHORT_FRAMES = 176
SHORT_HALO = 22
BEAM_LANES = 384


def dft_tables(length):
    k = np.arange(length)
    phases = (k[:, None] * k[None, :] % length) * (2.0 * math.pi / length)
    factor = 1.0 / math.sqrt(length)
    return np.cos(phases) * factor, np.sin(phases) * factor


def constant_tables():
    bf = ml_dtypes.bfloat16
    cos, sin = dft_tables(RADIX)
    order = np.concatenate([np.arange(0, RADIX, 2), np.arange(1, RADIX, 2)])
    c, s = cos[order].T, sin[order].T
    first = np.block([[c, s], [-s, c]])
    k = np.arange(RADIX)
    phases = (k[:, None] * k[None, :]) * (2.0 * math.pi / (RADIX * RADIX))
    twist = np.stack([np.tile(np.cos(phases), (1, 4)), np.tile(np.sin(phases), (1, 4))])
    second = np.zeros((RADIX, 4, 2, 2, 4, RADIX))
    for q in range(4):
        second[:, q, 0, 0, q] = cos.T
        second[:, q, 0, 1, q] = sin.T
        second[:, q, 1, 0, q] = -sin.T
        second[:, q, 1, 1, q] = cos.T
    second = second.reshape(512, 512)
    cos, sin = dft_tables(256)
    short = np.zeros((256, 2, 2, 256))
    short[:, 0, 0] = cos.T
    short[:, 0, 1] = sin.T
    short[:, 1, 0] = -sin.T
    short[:, 1, 1] = cos.T
    short = short.reshape(512, 512)
    pick = np.zeros((2, 384, 16, 2, 4, 2))
    for pair in range(2):
        for src in range(16):
            for q in range(4):
                u = src * 4 + q
                pick[pair, 2 * u, src, pair, q, 0] = 1
                pick[pair, 2 * u + 1, src, pair, q, 1] = 1
                pick[pair, 128 + 2 * u, src, pair, q, 1] = 1
                pick[pair, 128 + 2 * u + 1, src, pair, q, 0] = -1
                pick[pair, 256 + u, src, pair, q, 0] = 1
                pick[pair, 320 + u, src, pair, q, 1] = 1
    pick = pick.reshape(768, 256)
    return (
        first.astype(bf),
        twist.astype(np.float32),
        second.astype(bf),
        short.astype(bf),
        pick.astype(bf),
    )


def dot(a, b):
    return lax.dot_general(a, b, (((1,), (0,)), ((), ())), preferred_element_type=F32)


def dot_t(a, b):
    return lax.dot_general(a, b, (((1,), (1,)), ((), ())), preferred_element_type=F32)


def partner(stn, offset):
    y = lax.rem(stn // 32 + offset // 32, 2)
    z = lax.rem(lax.rem(stn // 4, 8) + lax.rem(offset // 4, 8), 8)
    x = lax.rem(lax.rem(stn, 4) + lax.rem(offset, 4), 4)
    return y * 32 + z * 4 + x


def kernel(
    x_ref, corr_taps, beam_taps, angles, index, first, twist, second, short, pick,
    vis_ref, power_ref,
    hist, ext, fs, fl, z_ref, tw, send_beam, recv_beam, send_spec, recv_spec,
    table, weights, lhs, rhs, part_own, part_send, part_recv,
    halo_send, halo_recv, beam_send_sem, beam_recv_sem, spec_send_sem, spec_recv_sem,
    part_send_sem, part_recv_sem, local_sem,
):
    stn = lax.axis_index("stn")
    grp = lax.axis_index("grp")

    barrier = pltpu.get_barrier_semaphore()

    def greet(k, _):
        pl.semaphore_signal(
            barrier, inc=1, device_id=(partner(stn, k), grp), device_id_type=MESH
        )
        return 0

    lax.fori_loop(1, STN, greet, 0)
    for k in range(1, GRP):
        pl.semaphore_signal(
            barrier, inc=1, device_id=(stn, lax.rem(grp + k, GRP)), device_id_type=MESH
        )

    def widen(source, at, first_tile):
        def body(i, _):
            v = source[i].astype(F32)
            ext[at + i] = v[:8]
            ext[at + HALF + i] = v[8:]
            return 0

        lax.fori_loop(first_tile, HALF, body, 0, unroll=8)

    widen(x_ref, TILES, 0)
    pl.semaphore_wait(barrier, STN - 1 + GRP - 1)

    def halo(i):
        at = pl.ds(HALF - SHORT_HALO, SHORT_HALO) if i == 0 else pl.ds(0, HALF - SHORT_HALO)
        return pltpu.make_async_remote_copy(
            src_ref=x_ref.at[at],
            dst_ref=hist.at[at],
            send_sem=halo_send.at[i],
            recv_sem=halo_recv.at[i],
            device_id=(stn, lax.rem(grp + 1, GRP)),
            device_id_type=MESH,
        )

    @pl.when(grp < GRP - 1)
    def _():
        halo(0).start()
        halo(1).start()

    @pl.when(grp == 0)
    def _():
        def clear(i, _):
            ext[i] = jnp.zeros((8, LANES), F32)
            return 0

        lax.fori_loop(0, TILES, clear, 0, unroll=8)

    @pl.when(grp > 0)
    def _():
        halo(0).wait_recv()
        widen(hist, 0, HALF - SHORT_HALO)

    step = 8

    def short_filter(i, _):
        for a in range(2):
            taps = [
                jnp.broadcast_to(beam_taps[pl.ds(k, 1), a * LANES : (a + 1) * LANES], (8, LANES))
                for k in range(TAPS)
            ]
            base = TILES + i * (2 * step) + a
            window = [ext[base + 2 * j] for j in range(1 - TAPS, step)]
            for f in range(step):
                total = window[f + TAPS - 1] * taps[0]
                for k in range(1, TAPS):
                    total = total + window[f + TAPS - 1 - k] * taps[k]
                fs[a, pl.ds(pl.multiple_of((i * step + f) * 8, 8), 8), :] = total
        return 0

    lax.fori_loop(0, SHORT_FRAMES // step, short_filter, 0)
    halves = []
    for st in range(2):
        for p in range(2):
            for part in range(2):
                for a in range(2):
                    z_ref[pl.ds(p * SHORT_FRAMES, SHORT_FRAMES), pl.ds(part * 256 + a * LANES, LANES)] = fs[
                        a, pl.ds(part * 4 + st * 2 + p, SHORT_FRAMES, stride=8), :
                    ].astype(BF)
        z_ref[pl.ds(2 * SHORT_FRAMES, BEAM_LANES - 2 * SHORT_FRAMES), :] = jnp.zeros(
            (BEAM_LANES - 2 * SHORT_FRAMES, 512), BF
        )
        halves.append(dot_t(short[...], z_ref[...]).reshape(STN, 8, BEAM_LANES))
    send_beam[...] = jnp.concatenate(halves, axis=1).astype(BF)

    def exchange(source, target, send_sem, recv_sem, k):
        other = partner(stn, k)
        return pltpu.make_async_remote_copy(
            src_ref=source.at[other],
            dst_ref=target.at[stn],
            send_sem=send_sem,
            recv_sem=recv_sem,
            device_id=(other, grp),
            device_id_type=MESH,
        )

    def send_all(source, target, send_sem, recv_sem):
        def body(k, _):
            exchange(source, target, send_sem, recv_sem, k).start()
            return 0

        lax.fori_loop(1, STN, body, 0)

    def wait_all(source, target, send_sem, recv_sem):
        span = pl.ds(0, STN - 1)
        pltpu.make_async_copy(source.at[span], target.at[span], recv_sem).wait()

    def wait_sent(source, target, send_sem, recv_sem):
        span = pl.ds(0, STN - 1)
        pltpu.make_async_copy(source.at[span], target.at[span], send_sem).wait()

    beam_args = (send_beam, recv_beam, beam_send_sem, beam_recv_sem)
    spec_args = (send_spec, recv_spec, spec_send_sem, spec_recv_sem)
    send_all(*beam_args)
    recv_beam[stn] = send_beam[stn]

    @pl.when(grp > 0)
    def _():
        halo(1).wait_recv()

        def body(i, _):
            v = hist[i].astype(F32)
            ext[i] = v[:8]
            ext[HALF + i] = v[8:]
            return 0

        lax.fori_loop(0, HALF - SHORT_HALO, body, 0, unroll=7)

    def long_filter(i, _):
        taps = [
            jnp.broadcast_to(
                corr_taps[pl.ds(k, 1), pl.ds(pl.multiple_of(i * LANES, LANES), LANES)], (8, LANES)
            )
            for k in range(TAPS)
        ]
        window = [ext[i + 32 * j] for j in range(2 * FRAMES)]
        for g in range(FRAMES):
            total = window[g + TAPS - 1] * taps[0]
            for k in range(1, TAPS):
                total = total + window[g + TAPS - 1 - k] * taps[k]
            fl[pl.ds(pl.multiple_of((g * 32 + i) * 8, 8), 8), :] = total
        return 0

    lax.fori_loop(0, 32, long_filter, 0)

    low = lax.broadcasted_iota(jnp.int32, (32, LANES), 1) < RADIX

    def first_factor(g, _):
        rows = []
        for part in range(2):
            even, odd = [], []
            for q2 in range(2):
                a = fl[pl.ds(g * 256 + part * 4 + 2 * q2, 32, stride=8), :]
                b = fl[pl.ds(g * 256 + part * 4 + 2 * q2 + 1, 32, stride=8), :]
                even.append(jnp.where(low, a, pltpu.roll(b, RADIX, 1)))
                odd.append(jnp.where(low, pltpu.roll(a, RADIX, 1), b))
            rows.append(jnp.concatenate(even, axis=1))
            rows.append(jnp.concatenate(odd, axis=1))
        out = dot(first[...], jnp.concatenate(rows, axis=0).astype(BF))
        real, imag = out[:RADIX], out[RADIX:]
        at = pl.ds(pl.multiple_of(g * RADIX, RADIX), RADIX)
        tw[at, 0:256] = (real * twist[0] + imag * twist[1]).astype(BF)
        tw[at, 256:512] = (imag * twist[0] - real * twist[1]).astype(BF)
        return 0

    lax.fori_loop(0, FRAMES, first_factor, 0)
    tw[FRAMES * RADIX : 12 * RADIX, :] = jnp.zeros((RADIX, 512), BF)

    for gpp in range(3):
        pairs = [
            dot_t(second[...], tw[(2 * gpp + e) * LANES : (2 * gpp + e + 1) * LANES, :]).reshape(STN, 8, LANES)
            for e in range(2)
        ]
        send_spec[:, 16 * gpp : 16 * gpp + 16, :] = jnp.concatenate(pairs, axis=1).astype(BF)

    send_all(*spec_args)
    recv_spec[stn] = send_spec[stn]

    shape = (256, 1024)
    column = lax.broadcasted_iota(jnp.int32, shape, 1)
    match = lax.broadcasted_iota(jnp.int32, shape, 0) == stn * 4 + (column // 2) % 4
    own_re = jnp.where(match & (column % 2 == 0), 1.0, 0.0).astype(BF)
    own_im = jnp.where(match & (column % 2 == 1), 1.0, 0.0).astype(BF)
    factor = 1.0 / math.sqrt(2 * STN)
    cos = (jnp.cos(angles[...]) * factor).astype(BF)
    sin = (jnp.sin(angles[...]) * factor).astype(BF)
    table[0] = dot(cos, own_re) - dot(sin, own_im)
    table[1] = dot(sin, own_re) + dot(cos, own_im)
    shape = (128, 1024)
    spread = jnp.where(
        lax.broadcasted_iota(jnp.int32, shape, 0) == lax.broadcasted_iota(jnp.int32, shape, 1) // 8,
        1.0,
        0.0,
    ).astype(BF)
    chosen = dot(index[...].astype(F32).astype(BF), spread)

    def choose(t, carry):
        real, imag = carry
        hit = chosen == t.astype(F32)
        return (
            jnp.where(hit, jnp.broadcast_to(table[0, pl.ds(t, 1), :], (16, 1024)), real),
            jnp.where(hit, jnp.broadcast_to(table[1, pl.ds(t, 1), :], (16, 1024)), imag),
        )

    zero = jnp.zeros((16, 1024), F32)
    chosen_parts = lax.fori_loop(0, 64, choose, (zero, zero))
    channel = (lax.broadcasted_iota(jnp.int32, (16, 1024), 1) // 2) % 4
    for po in range(2):
        for ci in range(4):
            weights[po * 64 + ci * 16 : po * 64 + ci * 16 + 16, :] = jnp.where(
                channel == ci, chosen_parts[po], 0.0
            ).astype(BF)

    wait_all(*beam_args)
    fields = dot(weights[...], recv_beam[...].reshape(1024, BEAM_LANES))
    power = fields[:64] * fields[:64] + fields[64:] * fields[64:]
    power_ref[...] = power[:, 0:SHORT_FRAMES] + power[:, SHORT_FRAMES : 2 * SHORT_FRAMES]

    wait_all(*spec_args)

    def gather_rows(b, _):
        for gpp in range(3):
            block = recv_spec[pl.ds(b * 16, 16), 16 * gpp : 16 * gpp + 16, :].reshape(256, LANES)
            rows = dot(pick[...], block).astype(BF)
            for e in range(2):
                at = 384 * e
                lanes = (2 * gpp + e) * LANES
                wide = pl.ds(pl.multiple_of(b * 128, 128), 128)
                narrow = pl.ds(pl.multiple_of(b * 64, 64), 64)
                lhs[wide, lanes : lanes + LANES] = rows[at : at + 128]
                lhs[wide, 768 + lanes : 768 + lanes + LANES] = rows[at + 128 : at + 256]
                rhs[narrow, lanes : lanes + LANES] = rows[at + 256 : at + 320]
                rhs[narrow, 768 + lanes : 768 + lanes + LANES] = rows[at + 320 : at + 384]
        return 0

    lax.fori_loop(0, 4, gather_rows, 0)
    for i in range(GRP):
        partial = dot_t(lhs[i * 128 : i * 128 + 128, :], rhs[...])
        part_own[i] = partial
        part_send[i] = partial.astype(BF)

    def hand_over(k):
        other = lax.rem(grp + k, GRP)
        return pltpu.make_async_remote_copy(
            src_ref=part_send.at[other],
            dst_ref=part_recv.at[k - 1],
            send_sem=part_send_sem.at[k - 1],
            recv_sem=part_recv_sem.at[k - 1],
            device_id=(stn, other),
            device_id_type=MESH,
        )

    for k in range(1, GRP):
        hand_over(k).start()
    total = part_own[grp]
    for k in range(1, GRP):
        hand_over(k).wait_recv()
        total = total + part_recv[k - 1].astype(F32)
    vis_ref[...] = total * (1.0 / math.sqrt(4 * FRAMES * RADIX))

    for k in range(1, GRP):
        hand_over(k).wait_send()
    wait_sent(*beam_args)
    wait_sent(*spec_args)

    @pl.when(grp < GRP - 1)
    def _():
        halo(0).wait_send()
        halo(1).wait_send()


def on_device(voltages, corr_taps, beam_taps, angle_table, table_index):
    x = voltages.reshape(8, 2, HALF, LANES).transpose(2, 1, 0, 3).reshape(HALF, 16, LANES)
    tables = [jnp.asarray(t) for t in constant_tables()]
    vmem = pl.BlockSpec(memory_space=pltpu.VMEM)
    dma = pltpu.SemaphoreType.DMA
    vis, power = pl.pallas_call(
        kernel,
        out_shape=(
            jax.ShapeDtypeStruct((128, 256), F32),
            jax.ShapeDtypeStruct((64, SHORT_FRAMES), F32),
        ),
        in_specs=[vmem] * 10,
        out_specs=(vmem, vmem),
        scratch_shapes=[
            pltpu.VMEM((HALF, 16, LANES), BF),
            pltpu.VMEM((2 * TILES, 8, LANES), F32),
            pltpu.VMEM((2, SHORT_FRAMES * 8, LANES), F32),
            pltpu.VMEM((FRAMES * 256, LANES), F32),
            pltpu.VMEM((BEAM_LANES, 512), BF),
            pltpu.VMEM((12 * RADIX, 512), BF),
            pltpu.VMEM((STN, 16, BEAM_LANES), BF),
            pltpu.VMEM((STN, 16, BEAM_LANES), BF),
            pltpu.VMEM((STN, 48, LANES), BF),
            pltpu.VMEM((STN, 48, LANES), BF),
            pltpu.VMEM((2, 64, 1024), F32),
            pltpu.VMEM((128, 1024), BF),
            pltpu.VMEM((512, 1536), BF),
            pltpu.VMEM((256, 1536), BF),
            pltpu.VMEM((GRP, 128, 256), F32),
            pltpu.VMEM((GRP, 128, 256), BF),
            pltpu.VMEM((GRP - 1, 128, 256), BF),
            dma((2,)),
            dma((2,)),
            dma,
            dma,
            dma,
            dma,
            dma((GRP - 1,)),
            dma((GRP - 1,)),
            dma,
        ],
        compiler_params=pltpu.CompilerParams(
            collective_id=0, has_side_effects=True, vmem_limit_bytes=48 * 1024 * 1024
        ),
    )(x, corr_taps, beam_taps, angle_table, table_index, *tables)
    return vis.reshape(1, 64, 2, 256), power.reshape(4, 16, SHORT_FRAMES)


def solution(mesh):
    in_specs = (P(None, "stn", None, "grp"), P(), P(), P(), P())
    out_specs = (P("stn", "grp", None, None), P("stn", None, "grp"))
    return jax.shard_map(
        on_device, mesh=mesh, in_specs=in_specs, out_specs=out_specs, check_vma=False
    )
```

time: 197 us -> 67.4 us (0.34)
  local copies, waits for them, and re-layouts: 91.7 us -> 4.22 us
  Pallas kernels: 0 us -> 62.3 us
  waiting for transfers between devices: 32.6 us -> 0 us
  starting transfers between devices: 31.5 us -> 0 us
  matrix products: 16.5 us -> 0 us
  between operations: 14.5 us -> 0.77 us
  other arithmetic: 8.7 us -> 0 us
    pallas_call x0 -> x1, Pallas kernels: none -> 62.3 us  [on_device(): pl.pallas_call(kernel, out_shape=(jax.ShapeDtypeStruct((128, 256), F32),...]
    unnamed x34 -> x19, local copies, waits for them, and re-layouts: 36 us -> 1.6 us
    all_to_all x2 -> x0, starting transfers between devices: 26.5 us -> none  [the longest x1 14.2 us: on_device(): lax.all_to_all(short_spectra.transpose(4, 0, 1, 2, 3), 'stn', split_axis=...]
    another operation x9 -> x0, local copies, waits for them, and re-layouts: 21.9 us -> none  [the longest x5 19.1 us: long_transform(): jnp.stack([result_real.astype(jnp.bfloat16).reshape(flat_shape), result_i...]
    all_to_all x2 -> x0, local copies, waits for them, and re-layouts: 21.7 us -> none  [the longest x1 19.8 us: on_device(): lax.all_to_all(spectra, 'stn', split_axis=4, concat_axis=1, tiled=True)]
    all_to_all x2 -> x0, waiting for transfers between devices: 16.8 us -> none  [the longest x1 16.8 us: on_device(): lax.all_to_all(spectra, 'stn', split_axis=4, concat_axis=1, tiled=True)]
    dot_general x19 -> x0, matrix products: 16.5 us -> none  [the longest x16 15.1 us: contract(): jnp.einsum(pattern, left_side, right_side, preferred_element_type=jnp.flo...]
    reduce_scatter x1 -> x0, waiting for transfers between devices: 11.2 us -> none  [on_device(): lax.psum_scatter(jnp.stack([real_part, imag_part], 1), 'grp', scatter_dim...]
  transfers between devices with their start and end apart: 4 -> 0, of which waited for: 3 -> 0; matrix products, arithmetic and copies ran while one was open for 25% -> 0% of each run, Pallas kernels for 0% -> 0%
where the time goes in v2:
time: 67.4 us; the launch traced here: 67.3 us
  Pallas kernels  62.3 us (92%)
  local copies, waits for them, and re-layouts  4.22 us (6%)
  between operations  0.77 us (1%)
    pallas_call x1, Pallas kernels, on_device(): pl.pallas_call(kernel, out_shape=(jax.ShapeDtypeStruct((128, 256), F32),...  62.3 us
    reshape x2, local copies, waits for them, and re-layouts, on_device(): voltages.reshape(8, 2, HALF, LANES).transpose(2, 1, 0, 3)  1.89 us
    unnamed x19, local copies, waits for them, and re-layouts  1.6 us

profile of v2, /device:TPU:1, one launch (start us, length us, event | category | flops | bytes accessed | tf_op | source)
XLA Modules:
  0.0 67.3 jit_solution(18043677874623416171)
XLA Ops:
  0.6 0.0 copy-start.3
  0.6 0.0 copy-start.4
  0.7 0.0 copy-start.5
  0.7 0.0 copy-start.6
  0.7 0.0 copy-start.7
  0.7 0.0 copy-start.8
  0.7 1.6 %reshape.16 = bf16[8,2,176,128]{3,2,1,0:T(8,128)(2,1)S(1)} reshape(bf16[2,2,2,45056]{3,2,1,0:T(2,128)(2,1)} %param.10) | data formatting | bytes 1441792 | tf_op jit(solution)/shard_map/reshape | solution.py:381
  2.3 0.0 copy-start
  2.3 0.0 copy-start.1
  2.3 0.0 copy-start.2
  2.3 0.3 copy.14
  2.6 0.0 copy-done.3
  2.6 0.0 copy-done.4
  2.7 0.0 copy-done.5
  2.7 0.0 copy-done.6
  2.7 0.0 copy-done.7
  2.7 0.0 copy-done.8
  2.7 0.7 copy-done
  3.4 0.2 copy-done.1
  3.5 0.1 copy-done.2
  3.6 62.3 %shard_map.113 = (f32[128,256]{1,0:T(8,128)S(1)}, f32[64,176]{1,0:T(8,128)S(1)}) custom-call(bf16[176,16,128]{2,1,0:T(8,128)(2,1)S(1)} %bitcast.6, f32[12,4096]{1,0:T(8,128)S(1)} %copy-done.3, f32[12,256]{1,0:T(8,128)S(1)} %copy-done.7, f32[64,256]{1,0:T(8,128)S(1)} %copy-done.5, s32[16,128]{1,0:T(8,128)S(1)} %copy-done.8, bf16[128,128]{1,0:T(8,128)(2,1)S(1)} %copy-done.6, ...), custom_call_target="tpu_custom_call" | custom-call | tf_op jit(solution)/shard_map/pallas_call | solution.py:385
  65.9 0.7 %reshape.18 = f32[1,64,2,256]{3,2,1,0:T(2,128)} reshape(f32[128,256]{1,0:T(8,128)S(1)} %get-tuple-element.4) | data formatting | bytes 262144 | tf_op jit(solution)/shard_map/reshape | solution.py:425
  66.6 0.6 copy.16
Async XLA Ops:
  0.6 2.0 %copy-start.3 = (f32[12,4096]{1,0:T(8,128)S(1)}, f32[12,4096]{1,0:T(8,128)}, u32[]{:S(2)}) copy-start(f32[12,4096]{1,0:T(8,128)} %corr_taps.1) | copy-start | bytes 589828
  0.6 2.0 %copy-start.4 = (f32[2,64,256]{2,1,0:T(8,128)S(1)}, f32[2,64,256]{2,1,0:T(8,128)}, u32[]{:S(2)}) copy-start(f32[2,64,256]{2,1,0:T(8,128)} %constant.11.clone.twist) | copy-start | bytes 393220
  0.7 2.0 %copy-start.5 = (f32[64,256]{1,0:T(8,128)S(1)}, f32[64,256]{1,0:T(8,128)}, u32[]{:S(2)}) copy-start(f32[64,256]{1,0:T(8,128)} %angles.1) | copy-start | bytes 196612
  0.7 2.0 %copy-start.6 = (bf16[128,128]{1,0:T(8,128)(2,1)S(1)}, bf16[128,128]{1,0:T(8,128)(2,1)}, u32[]{:S(2)}) copy-start(bf16[128,128]{1,0:T(8,128)(2,1)} %constant.10.clone.first) | copy-start | bytes 98308
  0.7 2.0 %copy-start.7 = (f32[12,256]{1,0:T(8,128)S(1)}, f32[12,256]{1,0:T(8,128)}, u32[]{:S(2)}) copy-start(f32[12,256]{1,0:T(8,128)} %beam_taps.1) | copy-start | bytes 36868
  0.7 2.0 %copy-start.8 = (s32[16,128]{1,0:T(8,128)S(1)}, s32[16,128]{1,0:T(8,128)}, u32[]{:S(2)}) copy-start(s32[16,128]{1,0:T(8,128)} %index.1) | copy-start | bytes 24580
  2.3 1.0 %copy-start = (bf16[512,512]{1,0:T(8,128)(2,1)S(1)}, bf16[512,512]{1,0:T(8,128)(2,1)}, u32[]{:S(2)}) copy-start(bf16[512,512]{1,0:T(8,128)(2,1)} %constant.13.clone.short) | copy-start | bytes 1572868
  2.3 1.2 %copy-start.1 = (bf16[512,512]{1,0:T(8,128)(2,1)S(1)}, bf16[512,512]{1,0:T(8,128)(2,1)}, u32[]{:S(2)}) copy-start(bf16[512,512]{1,0:T(8,128)(2,1)} %constant.12.clone.second) | copy-start | bytes 1572868
  2.3 1.3 %copy-start.2 = (bf16[768,256]{1,0:T(8,128)(2,1)S(1)}, bf16[768,256]{1,0:T(8,128)(2,1)}, u32[]{:S(2)}) copy-start(bf16[768,256]{1,0:T(8,128)(2,1)} %constant.14.clone.pick) | copy-start | bytes 1179652

commit v3 on v2

--- a/solution.py
+++ b/solution.py
@@ -23,8 +23,8 @@
 HALF = 176
 FRAMES = 11
 SHORT_FRAMES = 176
-SHORT_HALO = 22
-BEAM_LANES = 384
+FRAMES_B = 48
+FRAMES_A = SHORT_FRAMES - FRAMES_B
 
 
 def dft_tables(length):
@@ -94,70 +94,43 @@
 
 
 def kernel(
-    x_ref, corr_taps, beam_taps, angles, index, first, twist, second, short, pick,
+    x_ref, corr_taps, beam_taps, angles, index, first, twist, second_hbm, short_hbm, pick_hbm,
     vis_ref, power_ref,
-    hist, ext, fs, fl, z_ref, tw, send_beam, recv_beam, send_spec, recv_spec,
+    second, short, pick,
+    hist, ext, fs, fl, z_ref, tw, send_a, recv_a, send_b, recv_b, send_spec, recv_spec,
     table, weights, lhs, rhs, part_own, part_send, part_recv,
-    halo_send, halo_recv, beam_send_sem, beam_recv_sem, spec_send_sem, spec_recv_sem,
-    part_send_sem, part_recv_sem, local_sem,
+    row_sem, column_sem, table_sem, halo_send, halo_recv,
+    a_send_sem, a_recv_sem, b_send_sem, b_recv_sem, spec_send_sem, spec_recv_sem,
+    part_send_sem, part_recv_sem,
 ):
     stn = lax.axis_index("stn")
     grp = lax.axis_index("grp")
 
     barrier = pltpu.get_barrier_semaphore()
-
-    def greet(k, _):
-        pl.semaphore_signal(
-            barrier, inc=1, device_id=(partner(stn, k), grp), device_id_type=MESH
-        )
-        return 0
-
-    lax.fori_loop(1, STN, greet, 0)
+    lines = (1, 2, 3, 4, 8, 12, 16, 20, 24, 28, 32)
     for k in range(1, GRP):
         pl.semaphore_signal(
             barrier, inc=1, device_id=(stn, lax.rem(grp + k, GRP)), device_id_type=MESH
         )
-
-    def widen(source, at, first_tile):
-        def body(i, _):
-            v = source[i].astype(F32)
-            ext[at + i] = v[:8]
-            ext[at + HALF + i] = v[8:]
-            return 0
-
-        lax.fori_loop(first_tile, HALF, body, 0, unroll=8)
-
-    widen(x_ref, TILES, 0)
-    pl.semaphore_wait(barrier, STN - 1 + GRP - 1)
-
-    def halo(i):
-        at = pl.ds(HALF - SHORT_HALO, SHORT_HALO) if i == 0 else pl.ds(0, HALF - SHORT_HALO)
-        return pltpu.make_async_remote_copy(
-            src_ref=x_ref.at[at],
-            dst_ref=hist.at[at],
-            send_sem=halo_send.at[i],
-            recv_sem=halo_recv.at[i],
-            device_id=(stn, lax.rem(grp + 1, GRP)),
-            device_id_type=MESH,
-        )
-
-    @pl.when(grp < GRP - 1)
-    def _():
-        halo(0).start()
-        halo(1).start()
-
-    @pl.when(grp == 0)
-    def _():
-        def clear(i, _):
-            ext[i] = jnp.zeros((8, LANES), F32)
-            return 0
-
-        lax.fori_loop(0, TILES, clear, 0, unroll=8)
-
-    @pl.when(grp > 0)
-    def _():
-        halo(0).wait_recv()
-        widen(hist, 0, HALF - SHORT_HALO)
+    for k in lines:
+        pl.semaphore_signal(
+            barrier, inc=1, device_id=(partner(stn, k), grp), device_id_type=MESH
+        )
+
+    def load(i):
+        source, target = ((short_hbm, short), (second_hbm, second), (pick_hbm, pick))[i]
+        return pltpu.make_async_copy(source, target, table_sem.at[i])
+
+    for i in range(3):
+        load(i).start()
+
+    def widen_own(i, _):
+        v = x_ref[i // 16, lax.rem(i, 16)].astype(F32)
+        ext[TILES + i] = v[:8]
+        ext[TILES + HALF + i] = v[8:]
+        return 0
+
+    lax.fori_loop(0, HALF, widen_own, 0, unroll=8)
 
     step = 8
 
@@ -176,20 +149,51 @@
                 fs[a, pl.ds(pl.multiple_of((i * step + f) * 8, 8), 8), :] = total
         return 0
 
-    lax.fori_loop(0, SHORT_FRAMES // step, short_filter, 0)
-    halves = []
-    for st in range(2):
-        for p in range(2):
-            for part in range(2):
-                for a in range(2):
-                    z_ref[pl.ds(p * SHORT_FRAMES, SHORT_FRAMES), pl.ds(part * 256 + a * LANES, LANES)] = fs[
-                        a, pl.ds(part * 4 + st * 2 + p, SHORT_FRAMES, stride=8), :
-                    ].astype(BF)
-        z_ref[pl.ds(2 * SHORT_FRAMES, BEAM_LANES - 2 * SHORT_FRAMES), :] = jnp.zeros(
-            (BEAM_LANES - 2 * SHORT_FRAMES, 512), BF
-        )
-        halves.append(dot_t(short[...], z_ref[...]).reshape(STN, 8, BEAM_LANES))
-    send_beam[...] = jnp.concatenate(halves, axis=1).astype(BF)
+    def short_spectra(first_frame, frames, target):
+        lanes = target.shape[-1]
+        halves = []
+        for st in range(2):
+            for p in range(2):
+                for part in range(2):
+                    for a in range(2):
+                        z_ref[pl.ds(p * frames, frames), pl.ds(part * 256 + a * LANES, LANES)] = fs[
+                            a, pl.ds(first_frame * 8 + part * 4 + st * 2 + p, frames, stride=8), :
+                        ].astype(BF)
+            if lanes > 2 * frames:
+                z_ref[pl.ds(2 * frames, lanes - 2 * frames), :] = jnp.zeros(
+                    (lanes - 2 * frames, 512), BF
+                )
+            halves.append(dot_t(short[...], z_ref[pl.ds(0, lanes), :]).reshape(STN, 8, lanes))
+        target[...] = jnp.concatenate(halves, axis=1).astype(BF)
+
+    lax.fori_loop(FRAMES_B // step, SHORT_FRAMES // step, short_filter, 0)
+
+    pl.semaphore_wait(barrier, len(lines) + GRP - 1)
+
+    def halo(c):
+        return pltpu.make_async_remote_copy(
+            src_ref=x_ref.at[:, pl.ds(4 * c, 4)],
+            dst_ref=hist.at[:, pl.ds(4 * c, 4)],
+            send_sem=halo_send.at[c],
+            recv_sem=halo_recv.at[c],
+            device_id=(stn, lax.rem(grp + 1, GRP)),
+            device_id_type=MESH,
+        )
+
+    @pl.when(grp < GRP - 1)
+    def _():
+        for c in range(4):
+            halo(c).start()
+
+    for k in (1, 2, 3):
+        pl.semaphore_signal(row_sem, inc=1, device_id=(partner(stn, k), grp), device_id_type=MESH)
+
+    load(0).wait()
+    short_spectra(FRAMES_B, FRAMES_A, send_a)
+
+    pl.semaphore_wait(row_sem, 3)
+    pl.semaphore_signal(column_sem, inc=1, device_id=(partner(stn, 32), grp), device_id_type=MESH)
+    pl.semaphore_wait(column_sem, 1)
 
     def exchange(source, target, send_sem, recv_sem, k):
         other = partner(stn, k)
@@ -208,6 +212,7 @@
             return 0
 
         lax.fori_loop(1, STN, body, 0)
+        target[stn] = source[stn]
 
     def wait_all(source, target, send_sem, recv_sem):
         span = pl.ds(0, STN - 1)
@@ -217,39 +222,51 @@
         span = pl.ds(0, STN - 1)
         pltpu.make_async_copy(source.at[span], target.at[span], send_sem).wait()
 
-    beam_args = (send_beam, recv_beam, beam_send_sem, beam_recv_sem)
+    a_args = (send_a, recv_a, a_send_sem, a_recv_sem)
+    b_args = (send_b, recv_b, b_send_sem, b_recv_sem)
     spec_args = (send_spec, recv_spec, spec_send_sem, spec_recv_sem)
-    send_all(*beam_args)
-    recv_beam[stn] = send_beam[stn]
-
-    @pl.when(grp > 0)
+    send_all(*a_args)
+
+    @pl.when(grp == 0)
     def _():
-        halo(1).wait_recv()
-
-        def body(i, _):
-            v = hist[i].astype(F32)
-            ext[i] = v[:8]
-            ext[HALF + i] = v[8:]
+        def clear(i, _):
+            ext[i] = jnp.zeros((8, LANES), F32)
             return 0
 
-        lax.fori_loop(0, HALF - SHORT_HALO, body, 0, unroll=7)
-
-    def long_filter(i, _):
-        taps = [
-            jnp.broadcast_to(
-                corr_taps[pl.ds(k, 1), pl.ds(pl.multiple_of(i * LANES, LANES), LANES)], (8, LANES)
-            )
-            for k in range(TAPS)
-        ]
-        window = [ext[i + 32 * j] for j in range(2 * FRAMES)]
-        for g in range(FRAMES):
-            total = window[g + TAPS - 1] * taps[0]
-            for k in range(1, TAPS):
-                total = total + window[g + TAPS - 1 - k] * taps[k]
-            fl[pl.ds(pl.multiple_of((g * 32 + i) * 8, 8), 8), :] = total
-        return 0
-
-    lax.fori_loop(0, 32, long_filter, 0)
+        lax.fori_loop(0, TILES, clear, 0, unroll=8)
+
+    for c in range(4):
+
+        @pl.when(grp > 0)
+        def _(c=c):
+            halo(c).wait_recv()
+
+            def body(i, _):
+                for j in range(4 * c, 4 * c + 4):
+                    v = hist[i, j].astype(F32)
+                    ext[i * 16 + j] = v[:8]
+                    ext[HALF + i * 16 + j] = v[8:]
+                return 0
+
+            lax.fori_loop(0, FRAMES, body, 0)
+
+        def long_filter(j, _, c=c):
+            i = 4 * c + lax.rem(j, 4) + 16 * (j // 4)
+            taps = [
+                jnp.broadcast_to(
+                    corr_taps[pl.ds(k, 1), pl.ds(pl.multiple_of(i * LANES, LANES), LANES)], (8, LANES)
+                )
+                for k in range(TAPS)
+            ]
+            window = [ext[i + 32 * m] for m in range(2 * FRAMES)]
+            for g in range(FRAMES):
+                total = window[g + TAPS - 1] * taps[0]
+                for k in range(1, TAPS):
+                    total = total + window[g + TAPS - 1 - k] * taps[k]
+                fl[pl.ds(pl.multiple_of((g * 32 + i) * 8, 8), 8), :] = total
+            return 0
+
+        lax.fori_loop(0, 8, long_filter, 0)
 
     low = lax.broadcasted_iota(jnp.int32, (32, LANES), 1) < RADIX
 
@@ -274,15 +291,18 @@
     lax.fori_loop(0, FRAMES, first_factor, 0)
     tw[FRAMES * RADIX : 12 * RADIX, :] = jnp.zeros((RADIX, 512), BF)
 
+    load(1).wait()
     for gpp in range(3):
         pairs = [
             dot_t(second[...], tw[(2 * gpp + e) * LANES : (2 * gpp + e + 1) * LANES, :]).reshape(STN, 8, LANES)
             for e in range(2)
         ]
         send_spec[:, 16 * gpp : 16 * gpp + 16, :] = jnp.concatenate(pairs, axis=1).astype(BF)
-
     send_all(*spec_args)
-    recv_spec[stn] = send_spec[stn]
+
+    lax.fori_loop(0, FRAMES_B // step, short_filter, 0)
+    short_spectra(0, FRAMES_B, send_b)
+    send_all(*b_args)
 
     shape = (256, 1024)
     column = lax.broadcasted_iota(jnp.int32, shape, 1)
@@ -319,11 +339,15 @@
                 channel == ci, chosen_parts[po], 0.0
             ).astype(BF)
 
-    wait_all(*beam_args)
-    fields = dot(weights[...], recv_beam[...].reshape(1024, BEAM_LANES))
-    power = fields[:64] * fields[:64] + fields[64:] * fields[64:]
-    power_ref[...] = power[:, 0:SHORT_FRAMES] + power[:, SHORT_FRAMES : 2 * SHORT_FRAMES]
-
+    def beam_power(source):
+        fields = dot(weights[...], source[...].reshape(1024, source.shape[-1]))
+        return fields[:64] * fields[:64] + fields[64:] * fields[64:]
+
+    wait_all(*a_args)
+    power = beam_power(recv_a)
+    power_ref[:, FRAMES_B:SHORT_FRAMES] = power[:, :FRAMES_A] + power[:, FRAMES_A:]
+
+    load(2).wait()
     wait_all(*spec_args)
 
     def gather_rows(b, _):
@@ -360,6 +384,11 @@
 
     for k in range(1, GRP):
         hand_over(k).start()
+
+    wait_all(*b_args)
+    power = beam_power(recv_b)
+    power_ref[:, 0:FRAMES_B] = power[:, :FRAMES_B] + power[:, FRAMES_B : 2 * FRAMES_B]
+
     total = part_own[grp]
     for k in range(1, GRP):
         hand_over(k).wait_recv()
@@ -368,17 +397,18 @@
 
     for k in range(1, GRP):
         hand_over(k).wait_send()
-    wait_sent(*beam_args)
+    wait_sent(*a_args)
     wait_sent(*spec_args)
+    wait_sent(*b_args)
 
     @pl.when(grp < GRP - 1)
     def _():
-        halo(0).wait_send()
-        halo(1).wait_send()
+        for c in range(4):
+            halo(c).wait_send()
 
 
 def on_device(voltages, corr_taps, beam_taps, angle_table, table_index):
-    x = voltages.reshape(8, 2, HALF, LANES).transpose(2, 1, 0, 3).reshape(HALF, 16, LANES)
+    x = voltages.reshape(8, 2, HALF, LANES).transpose(2, 1, 0, 3).reshape(FRAMES, 16, 16, LANES)
     tables = [jnp.asarray(t) for t in constant_tables()]
     vmem = pl.BlockSpec(memory_space=pltpu.VMEM)
     dma = pltpu.SemaphoreType.DMA
@@ -388,17 +418,22 @@
             jax.ShapeDtypeStruct((128, 256), F32),
             jax.ShapeDtypeStruct((64, SHORT_FRAMES), F32),
         ),
-        in_specs=[vmem] * 10,
+        in_specs=[vmem] * 7 + [pl.BlockSpec(memory_space=pl.ANY)] * 3,
         out_specs=(vmem, vmem),
         scratch_shapes=[
-            pltpu.VMEM((HALF, 16, LANES), BF),
+            pltpu.VMEM((512, 512), BF),
+            pltpu.VMEM((512, 512), BF),
+            pltpu.VMEM((768, 256), BF),
+            pltpu.VMEM((FRAMES, 16, 16, LANES), BF),
             pltpu.VMEM((2 * TILES, 8, LANES), F32),
             pltpu.VMEM((2, SHORT_FRAMES * 8, LANES), F32),
             pltpu.VMEM((FRAMES * 256, LANES), F32),
-            pltpu.VMEM((BEAM_LANES, 512), BF),
+            pltpu.VMEM((256, 512), BF),
             pltpu.VMEM((12 * RADIX, 512), BF),
-            pltpu.VMEM((STN, 16, BEAM_LANES), BF),
-            pltpu.VMEM((STN, 16, BEAM_LANES), BF),
+            pltpu.VMEM((STN, 16, 256), BF),
+            pltpu.VMEM((STN, 16, 256), BF),
+            pltpu.VMEM((STN, 16, LANES), BF),
+            pltpu.VMEM((STN, 16, LANES), BF),
             pltpu.VMEM((STN, 48, LANES), BF),
             pltpu.VMEM((STN, 48, LANES), BF),
             pltpu.VMEM((2, 64, 1024), F32),
@@ -408,15 +443,19 @@
             pltpu.VMEM((GRP, 128, 256), F32),
             pltpu.VMEM((GRP, 128, 256), BF),
             pltpu.VMEM((GRP - 1, 128, 256), BF),
-            dma((2,)),
-            dma((2,)),
+            pltpu.SemaphoreType.REGULAR,
+            pltpu.SemaphoreType.REGULAR,
+            dma((3,)),
+            dma((4,)),
+            dma((4,)),
+            dma,
+            dma,
             dma,
             dma,
             dma,
             dma,
             dma((GRP - 1,)),
             dma((GRP - 1,)),
-            dma,
         ],
         compiler_params=pltpu.CompilerParams(
             collective_id=0, has_side_effects=True, vmem_limit_bytes=48 * 1024 * 1024

time: 67.4 us -> 59.7 us (0.89)
  Pallas kernels: 62.3 us -> 54.6 us
    pallas_call x1, Pallas kernels: 62.3 us -> 54.6 us  [on_device(): pl.pallas_call(kernel, out_shape=(jax.ShapeDtypeStruct((128, 256), F32),...]
where the time goes in v3:
time: 59.7 us; the launch traced here: 59.6 us
  Pallas kernels  54.6 us (91%)
  local copies, waits for them, and re-layouts  4.22 us (7%)
  between operations  0.77 us (1%)
    pallas_call x1, Pallas kernels, on_device(): pl.pallas_call(kernel, out_shape=(jax.ShapeDtypeStruct((128, 256), F32),...  54.6 us
    reshape x2, local copies, waits for them, and re-layouts, on_device(): voltages.reshape(8, 2, HALF, LANES).transpose(2, 1, 0, 3)  1.89 us
    unnamed x19, local copies, waits for them, and re-layouts  1.6 us

profile of v3, /device:TPU:1, one launch (start us, length us, event | category | flops | bytes accessed | tf_op | source)
XLA Modules:
  0.0 59.6 jit_solution(15247160807123463101)
XLA Ops:
  0.6 0.0 copy-start.3
  0.6 0.0 copy-start.4
  0.7 0.0 copy-start.5
  0.7 0.0 copy-start.6
  0.7 0.0 copy-start.7
  0.7 0.0 copy-start.8
  0.7 1.6 %reshape.16 = bf16[8,2,176,128]{3,2,1,0:T(8,128)(2,1)S(1)} reshape(bf16[2,2,2,45056]{3,2,1,0:T(2,128)(2,1)} %param.10) | data formatting | bytes 1441792 | tf_op jit(solution)/shard_map/reshape | solution.py:411
  2.3 0.0 copy-start
  2.3 0.0 copy-start.1
  2.3 0.0 copy-start.2
  2.3 0.3 copy.12
  2.6 0.0 copy-done.3
  2.6 0.0 copy-done.4
  2.7 0.0 copy-done.5
  2.7 0.0 copy-done.6
  2.7 0.0 copy-done.7
  2.7 0.0 copy-done.8
  2.7 0.7 %copy-done = bf16[512,512]{1,0:T(8,128)(2,1)S(1)} copy-done((bf16[512,512]{1,0:T(8,128)(2,1)S(1)}, bf16[512,512]{1,0:T(8,128)(2,1)}, u32[]{:S(2)}) %copy-start) | copy-done | bytes 524312
  3.4 0.2 copy-done.1
  3.5 0.1 copy-done.2
  3.6 54.6 %shard_map.113 = (f32[128,256]{1,0:T(8,128)S(1)}, f32[64,176]{1,0:T(8,128)S(1)}) custom-call(bf16[11,16,16,128]{3,2,1,0:T(8,128)(2,1)S(1)} %bitcast.4, f32[12,4096]{1,0:T(8,128)S(1)} %copy-done.3, f32[12,256]{1,0:T(8,128)S(1)} %copy-done.7, f32[64,256]{1,0:T(8,128)S(1)} %copy-done.5, s32[16,128]{1,0:T(8,128)S(1)} %copy-done.8, ...), custom_call_target="tpu_custom_call" | custom-call | tf_op jit(solution)/shard_map/pallas_call | solution.py:415
  58.2 0.7 %reshape.18 = f32[1,64,2,256]{3,2,1,0:T(2,128)} reshape(f32[128,256]{1,0:T(8,128)S(1)} %get-tuple-element.4) | data formatting | bytes 262144 | tf_op jit(solution)/shard_map/reshape | solution.py:464
  59.0 0.6 %copy.14 = f32[4,16,176]{2,1,0:T(8,128)} copy(f32[4,16,176]{2,1,0:T(8,128)S(1)} %bitcast.5) | data formatting | bytes 90112
Async XLA Ops:
  0.6 2.0 %copy-start.3 = (f32[12,4096]{1,0:T(8,128)S(1)}, f32[12,4096]{1,0:T(8,128)}, u32[]{:S(2)}) copy-start(f32[12,4096]{1,0:T(8,128)} %corr_taps.1) | copy-start | bytes 589828
  0.6 2.0 %copy-start.4 = (f32[2,64,256]{2,1,0:T(8,128)S(1)}, f32[2,64,256]{2,1,0:T(8,128)}, u32[]{:S(2)}) copy-start(f32[2,64,256]{2,1,0:T(8,128)} %constant.11.clone.twist) | copy-start | bytes 393220
  0.7 2.0 %copy-start.5 = (f32[64,256]{1,0:T(8,128)S(1)}, f32[64,256]{1,0:T(8,128)}, u32[]{:S(2)}) copy-start(f32[64,256]{1,0:T(8,128)} %angles.1) | copy-start | bytes 196612
  0.7 2.0 %copy-start.6 = (bf16[128,128]{1,0:T(8,128)(2,1)S(1)}, bf16[128,128]{1,0:T(8,128)(2,1)}, u32[]{:S(2)}) copy-start(bf16[128,128]{1,0:T(8,128)(2,1)} %constant.10.clone.first) | copy-start | bytes 98308
  0.7 2.0 %copy-start.7 = (f32[12,256]{1,0:T(8,128)S(1)}, f32[12,256]{1,0:T(8,128)}, u32[]{:S(2)}) copy-start(f32[12,256]{1,0:T(8,128)} %beam_taps.1) | copy-start | bytes 36868
  0.7 2.0 %copy-start.8 = (s32[16,128]{1,0:T(8,128)S(1)}, s32[16,128]{1,0:T(8,128)}, u32[]{:S(2)}) copy-start(s32[16,128]{1,0:T(8,128)} %index.1) | copy-start | bytes 24580
  2.3 1.0 %copy-start = (bf16[512,512]{1,0:T(8,128)(2,1)S(1)}, bf16[512,512]{1,0:T(8,128)(2,1)}, u32[]{:S(2)}) copy-start(bf16[512,512]{1,0:T(8,128)(2,1)} %constant.13.clone.short_hbm) | copy-start | bytes 1572868
  2.3 1.2 %copy-start.1 = (bf16[512,512]{1,0:T(8,128)(2,1)S(1)}, bf16[512,512]{1,0:T(8,128)(2,1)}, u32[]{:S(2)}) copy-start(bf16[512,512]{1,0:T(8,128)(2,1)} %constant.12.clone.second_hbm) | copy-start | bytes 1572868
  2.3 1.3 %copy-start.2 = (bf16[768,256]{1,0:T(8,128)(2,1)S(1)}, bf16[768,256]{1,0:T(8,128)(2,1)}, u32[]{:S(2)}) copy-start(bf16[768,256]{1,0:T(8,128)(2,1)} %constant.14.clone.pick_hbm) | copy-start | bytes 1179652

commit v4 on v3

--- a/solution.py
+++ b/solution.py
@@ -24,6 +24,7 @@
 FRAMES = 11
 SHORT_FRAMES = 176
 FRAMES_B = 48
+GROUPS = ((8, 3), (4, 4), (0, 4))
 FRAMES_A = SHORT_FRAMES - FRAMES_B
 
 
@@ -125,9 +126,9 @@
         load(i).start()
 
     def widen_own(i, _):
-        v = x_ref[i // 16, lax.rem(i, 16)].astype(F32)
-        ext[TILES + i] = v[:8]
-        ext[TILES + HALF + i] = v[8:]
+        v = x_ref[i].astype(F32)
+        ext[TILES + 2 * i] = v[:8]
+        ext[TILES + 2 * i + 1] = v[8:]
         return 0
 
     lax.fori_loop(0, HALF, widen_own, 0, unroll=8)
@@ -167,13 +168,28 @@
         target[...] = jnp.concatenate(halves, axis=1).astype(BF)
 
     lax.fori_loop(FRAMES_B // step, SHORT_FRAMES // step, short_filter, 0)
+    load(0).wait()
+    short_spectra(FRAMES_B, FRAMES_A, send_a)
+
+    @pl.when(grp == 0)
+    def _():
+        def clear(i, _):
+            ext[i] = jnp.zeros((8, LANES), F32)
+            return 0
+
+        lax.fori_loop(0, TILES, clear, 0, unroll=8)
 
     pl.semaphore_wait(barrier, len(lines) + GRP - 1)
 
+    for k in (1, 2, 3):
+        pl.semaphore_signal(row_sem, inc=1, device_id=(partner(stn, k), grp), device_id_type=MESH)
+
     def halo(c):
+        first_frame, frames = GROUPS[c]
+        at = pl.ds(16 * first_frame, 16 * frames)
         return pltpu.make_async_remote_copy(
-            src_ref=x_ref.at[:, pl.ds(4 * c, 4)],
-            dst_ref=hist.at[:, pl.ds(4 * c, 4)],
+            src_ref=x_ref.at[at],
+            dst_ref=hist.at[at],
             send_sem=halo_send.at[c],
             recv_sem=halo_recv.at[c],
             device_id=(stn, lax.rem(grp + 1, GRP)),
@@ -182,18 +198,8 @@
 
     @pl.when(grp < GRP - 1)
     def _():
-        for c in range(4):
+        for c in range(3):
             halo(c).start()
-
-    for k in (1, 2, 3):
-        pl.semaphore_signal(row_sem, inc=1, device_id=(partner(stn, k), grp), device_id_type=MESH)
-
-    load(0).wait()
-    short_spectra(FRAMES_B, FRAMES_A, send_a)
-
-    pl.semaphore_wait(row_sem, 3)
-    pl.semaphore_signal(column_sem, inc=1, device_id=(partner(stn, 32), grp), device_id_type=MESH)
-    pl.semaphore_wait(column_sem, 1)
 
     def exchange(source, target, send_sem, recv_sem, k):
         other = partner(stn, k)
@@ -206,13 +212,14 @@
             device_id_type=MESH,
         )
 
-    def send_all(source, target, send_sem, recv_sem):
+    def send_all(source, target, send_sem, recv_sem, start=1, stop=STN):
         def body(k, _):
             exchange(source, target, send_sem, recv_sem, k).start()
             return 0
 
-        lax.fori_loop(1, STN, body, 0)
-        target[stn] = source[stn]
+        lax.fori_loop(start, stop, body, 0)
+        if start == 1:
+            target[stn] = source[stn]
 
     def wait_all(source, target, send_sem, recv_sem):
         span = pl.ds(0, STN - 1)
@@ -224,81 +231,78 @@
 
     a_args = (send_a, recv_a, a_send_sem, a_recv_sem)
     b_args = (send_b, recv_b, b_send_sem, b_recv_sem)
-    spec_args = (send_spec, recv_spec, spec_send_sem, spec_recv_sem)
-    send_all(*a_args)
-
-    @pl.when(grp == 0)
-    def _():
-        def clear(i, _):
-            ext[i] = jnp.zeros((8, LANES), F32)
-            return 0
-
-        lax.fori_loop(0, TILES, clear, 0, unroll=8)
-
-    for c in range(4):
+    spec_args = [
+        (send_spec.at[c], recv_spec.at[c], spec_send_sem.at[c], spec_recv_sem.at[c]) for c in range(3)
+    ]
+
+    pl.semaphore_wait(row_sem, 3)
+    pl.semaphore_signal(column_sem, inc=1, device_id=(partner(stn, 32), grp), device_id_type=MESH)
+    send_all(*a_args, 1, STN // 2)
+    pl.semaphore_wait(column_sem, 1)
+    send_all(*a_args, STN // 2, STN)
+
+    low = lax.broadcasted_iota(jnp.int32, (32, LANES), 1) < RADIX
+    tw[FRAMES * RADIX : 12 * RADIX, :] = jnp.zeros((RADIX, 512), BF)
+
+    for c, (first_frame, frames) in enumerate(GROUPS):
 
         @pl.when(grp > 0)
-        def _(c=c):
+        def _(c=c, first_frame=first_frame, frames=frames):
             halo(c).wait_recv()
 
             def body(i, _):
-                for j in range(4 * c, 4 * c + 4):
-                    v = hist[i, j].astype(F32)
-                    ext[i * 16 + j] = v[:8]
-                    ext[HALF + i * 16 + j] = v[8:]
+                v = hist[i].astype(F32)
+                ext[2 * i] = v[:8]
+                ext[2 * i + 1] = v[8:]
                 return 0
 
-            lax.fori_loop(0, FRAMES, body, 0)
-
-        def long_filter(j, _, c=c):
-            i = 4 * c + lax.rem(j, 4) + 16 * (j // 4)
+            lax.fori_loop(16 * first_frame, 16 * (first_frame + frames), body, 0, unroll=8)
+
+        def long_filter(i, _, first_frame=first_frame, frames=frames):
             taps = [
                 jnp.broadcast_to(
                     corr_taps[pl.ds(k, 1), pl.ds(pl.multiple_of(i * LANES, LANES), LANES)], (8, LANES)
                 )
                 for k in range(TAPS)
             ]
-            window = [ext[i + 32 * m] for m in range(2 * FRAMES)]
-            for g in range(FRAMES):
+            window = [ext[i + 32 * (first_frame + m)] for m in range(frames + TAPS - 1)]
+            for g in range(frames):
                 total = window[g + TAPS - 1] * taps[0]
                 for k in range(1, TAPS):
                     total = total + window[g + TAPS - 1 - k] * taps[k]
-                fl[pl.ds(pl.multiple_of((g * 32 + i) * 8, 8), 8), :] = total
+                fl[pl.ds(pl.multiple_of(((first_frame + g) * 32 + i) * 8, 8), 8), :] = total
             return 0
 
-        lax.fori_loop(0, 8, long_filter, 0)
-
-    low = lax.broadcasted_iota(jnp.int32, (32, LANES), 1) < RADIX
-
-    def first_factor(g, _):
-        rows = []
-        for part in range(2):
-            even, odd = [], []
-            for q2 in range(2):
-                a = fl[pl.ds(g * 256 + part * 4 + 2 * q2, 32, stride=8), :]
-                b = fl[pl.ds(g * 256 + part * 4 + 2 * q2 + 1, 32, stride=8), :]
-                even.append(jnp.where(low, a, pltpu.roll(b, RADIX, 1)))
-                odd.append(jnp.where(low, pltpu.roll(a, RADIX, 1), b))
-            rows.append(jnp.concatenate(even, axis=1))
-            rows.append(jnp.concatenate(odd, axis=1))
-        out = dot(first[...], jnp.concatenate(rows, axis=0).astype(BF))
-        real, imag = out[:RADIX], out[RADIX:]
-        at = pl.ds(pl.multiple_of(g * RADIX, RADIX), RADIX)
-        tw[at, 0:256] = (real * twist[0] + imag * twist[1]).astype(BF)
-        tw[at, 256:512] = (imag * twist[0] - real * twist[1]).astype(BF)
-        return 0
-
-    lax.fori_loop(0, FRAMES, first_factor, 0)
-    tw[FRAMES * RADIX : 12 * RADIX, :] = jnp.zeros((RADIX, 512), BF)
-
-    load(1).wait()
-    for gpp in range(3):
+        lax.fori_loop(0, 32, long_filter, 0)
+
+        def first_factor(g, _):
+            rows = []
+            for part in range(2):
+                even, odd = [], []
+                for q2 in range(2):
+                    a = fl[pl.ds(g * 256 + part * 4 + 2 * q2, 32, stride=8), :]
+                    b = fl[pl.ds(g * 256 + part * 4 + 2 * q2 + 1, 32, stride=8), :]
+                    even.append(jnp.where(low, a, pltpu.roll(b, RADIX, 1)))
+                    odd.append(jnp.where(low, pltpu.roll(a, RADIX, 1), b))
+                rows.append(jnp.concatenate(even, axis=1))
+                rows.append(jnp.concatenate(odd, axis=1))
+            out = dot(first[...], jnp.concatenate(rows, axis=0).astype(BF))
+            real, imag = out[:RADIX], out[RADIX:]
+            at = pl.ds(pl.multiple_of(g * RADIX, RADIX), RADIX)
+            tw[at, 0:256] = (real * twist[0] + imag * twist[1]).astype(BF)
+            tw[at, 256:512] = (imag * twist[0] - real * twist[1]).astype(BF)
+            return 0
+
+        lax.fori_loop(first_frame, first_frame + frames, first_factor, 0)
+
+        if c == 0:
+            load(1).wait()
         pairs = [
-            dot_t(second[...], tw[(2 * gpp + e) * LANES : (2 * gpp + e + 1) * LANES, :]).reshape(STN, 8, LANES)
-            for e in range(2)
+            dot_t(second[...], tw[at : at + LANES, :]).reshape(STN, 8, LANES)
+            for at in (first_frame * RADIX, first_frame * RADIX + LANES)
         ]
-        send_spec[:, 16 * gpp : 16 * gpp + 16, :] = jnp.concatenate(pairs, axis=1).astype(BF)
-    send_all(*spec_args)
+        send_spec[c] = jnp.concatenate(pairs, axis=1).astype(BF)
+        send_all(*spec_args[c])
 
     lax.fori_loop(0, FRAMES_B // step, short_filter, 0)
     short_spectra(0, FRAMES_B, send_b)
@@ -347,30 +351,6 @@
     power = beam_power(recv_a)
     power_ref[:, FRAMES_B:SHORT_FRAMES] = power[:, :FRAMES_A] + power[:, FRAMES_A:]
 
-    load(2).wait()
-    wait_all(*spec_args)
-
-    def gather_rows(b, _):
-        for gpp in range(3):
-            block = recv_spec[pl.ds(b * 16, 16), 16 * gpp : 16 * gpp + 16, :].reshape(256, LANES)
-            rows = dot(pick[...], block).astype(BF)
-            for e in range(2):
-                at = 384 * e
-                lanes = (2 * gpp + e) * LANES
-                wide = pl.ds(pl.multiple_of(b * 128, 128), 128)
-                narrow = pl.ds(pl.multiple_of(b * 64, 64), 64)
-                lhs[wide, lanes : lanes + LANES] = rows[at : at + 128]
-                lhs[wide, 768 + lanes : 768 + lanes + LANES] = rows[at + 128 : at + 256]
-                rhs[narrow, lanes : lanes + LANES] = rows[at + 256 : at + 320]
-                rhs[narrow, 768 + lanes : 768 + lanes + LANES] = rows[at + 320 : at + 384]
-        return 0
-
-    lax.fori_loop(0, 4, gather_rows, 0)
-    for i in range(GRP):
-        partial = dot_t(lhs[i * 128 : i * 128 + 128, :], rhs[...])
-        part_own[i] = partial
-        part_send[i] = partial.astype(BF)
-
     def hand_over(k):
         other = lax.rem(grp + k, GRP)
         return pltpu.make_async_remote_copy(
@@ -382,14 +362,41 @@
             device_id_type=MESH,
         )
 
-    for k in range(1, GRP):
-        hand_over(k).start()
+    load(2).wait()
+    for c in range(3):
+        wait_all(*spec_args[c])
+
+        def gather_rows(b, _, c=c):
+            block = recv_spec[c, pl.ds(b * 16, 16)].reshape(256, LANES)
+            rows = dot(pick[...], block).astype(BF)
+            wide = pl.ds(pl.multiple_of(b * 128, 128), 128)
+            narrow = pl.ds(pl.multiple_of(b * 64, 64), 64)
+            for e in range(2):
+                at = 384 * e
+                lanes = 2 * e * LANES
+                lhs[wide, lanes : lanes + LANES] = rows[at : at + 128]
+                lhs[wide, lanes + LANES : lanes + 2 * LANES] = rows[at + 128 : at + 256]
+                rhs[narrow, lanes : lanes + LANES] = rows[at + 256 : at + 320]
+                rhs[narrow, lanes + LANES : lanes + 2 * LANES] = rows[at + 320 : at + 384]
+            return 0
+
+        lax.fori_loop(0, 4, gather_rows, 0)
+        for k in (1, 2, 3, 0):
+            owner = lax.rem(grp + k, GRP)
+            partial = dot_t(lhs[pl.ds(pl.multiple_of(owner * 128, 128), 128), :], rhs[...])
+            if c > 0:
+                partial = partial + part_own[k]
+            if c < 2 or k == 0:
+                part_own[k] = partial
+            else:
+                part_send[owner] = partial.astype(BF)
+                hand_over(k).start()
 
     wait_all(*b_args)
     power = beam_power(recv_b)
     power_ref[:, 0:FRAMES_B] = power[:, :FRAMES_B] + power[:, FRAMES_B : 2 * FRAMES_B]
 
-    total = part_own[grp]
+    total = part_own[0]
     for k in range(1, GRP):
         hand_over(k).wait_recv()
         total = total + part_recv[k - 1].astype(F32)
@@ -398,17 +405,18 @@
     for k in range(1, GRP):
         hand_over(k).wait_send()
     wait_sent(*a_args)
-    wait_sent(*spec_args)
+    for c in range(3):
+        wait_sent(*spec_args[c])
     wait_sent(*b_args)
 
     @pl.when(grp < GRP - 1)
     def _():
-        for c in range(4):
+        for c in range(3):
             halo(c).wait_send()
 
 
 def on_device(voltages, corr_taps, beam_taps, angle_table, table_index):
-    x = voltages.reshape(8, 2, HALF, LANES).transpose(2, 1, 0, 3).reshape(FRAMES, 16, 16, LANES)
+    x = voltages.reshape(8, TILES, LANES).transpose(1, 0, 2).reshape(HALF, 16, LANES)
     tables = [jnp.asarray(t) for t in constant_tables()]
     vmem = pl.BlockSpec(memory_space=pltpu.VMEM)
     dma = pltpu.SemaphoreType.DMA
@@ -418,13 +426,13 @@
             jax.ShapeDtypeStruct((128, 256), F32),
             jax.ShapeDtypeStruct((64, SHORT_FRAMES), F32),
         ),
-        in_specs=[vmem] * 7 + [pl.BlockSpec(memory_space=pl.ANY)] * 3,
+        in_specs=[vmem] * 7 + [pl.BlockSpec(memory_space=pltpu.HBM)] * 3,
         out_specs=(vmem, vmem),
         scratch_shapes=[
             pltpu.VMEM((512, 512), BF),
             pltpu.VMEM((512, 512), BF),
             pltpu.VMEM((768, 256), BF),
-            pltpu.VMEM((FRAMES, 16, 16, LANES), BF),
+            pltpu.VMEM((HALF, 16, LANES), BF),
             pltpu.VMEM((2 * TILES, 8, LANES), F32),
             pltpu.VMEM((2, SHORT_FRAMES * 8, LANES), F32),
             pltpu.VMEM((FRAMES * 256, LANES), F32),
@@ -434,26 +442,26 @@
             pltpu.VMEM((STN, 16, 256), BF),
             pltpu.VMEM((STN, 16, LANES), BF),
             pltpu.VMEM((STN, 16, LANES), BF),
-            pltpu.VMEM((STN, 48, LANES), BF),
-            pltpu.VMEM((STN, 48, LANES), BF),
+            pltpu.VMEM((3, STN, 16, LANES), BF),
+            pltpu.VMEM((3, STN, 16, LANES), BF),
             pltpu.VMEM((2, 64, 1024), F32),
             pltpu.VMEM((128, 1024), BF),
-            pltpu.VMEM((512, 1536), BF),
-            pltpu.VMEM((256, 1536), BF),
+            pltpu.VMEM((512, 512), BF),
+            pltpu.VMEM((256, 512), BF),
             pltpu.VMEM((GRP, 128, 256), F32),
             pltpu.VMEM((GRP, 128, 256), BF),
             pltpu.VMEM((GRP - 1, 128, 256), BF),
             pltpu.SemaphoreType.REGULAR,
             pltpu.SemaphoreType.REGULAR,
             dma((3,)),
-            dma((4,)),
-            dma((4,)),
+            dma((3,)),
+            dma((3,)),
             dma,
             dma,
             dma,
             dma,
-            dma,
-            dma,
+            dma((3,)),
+            dma((3,)),
             dma((GRP - 1,)),
             dma((GRP - 1,)),
         ],

time: 59.7 us -> 56.8 us (0.951)
  Pallas kernels: 54.6 us -> 51.7 us
    pallas_call x1, Pallas kernels: 54.6 us -> 51.7 us  [on_device(): pl.pallas_call(kernel, out_shape=(jax.ShapeDtypeStruct((128, 256), F32),...]
where the time goes in v4:
time: 56.8 us; the launch traced here: 56.7 us
  Pallas kernels  51.7 us (91%)
  local copies, waits for them, and re-layouts  4.22 us (7%)
  between operations  0.77 us (1%)
    pallas_call x1, Pallas kernels, on_device(): pl.pallas_call(kernel, out_shape=(jax.ShapeDtypeStruct((128, 256), F32),...  51.7 us
    reshape x2, local copies, waits for them, and re-layouts, on_device(): voltages.reshape(8, TILES, LANES).transpose(1, 0, 2)  1.89 us
    unnamed x19, local copies, waits for them, and re-layouts  1.6 us

profile of v4, /device:TPU:1, one launch (start us, length us, event | category | flops | bytes accessed | tf_op | source)
XLA Modules:
  0.0 56.7 jit_solution(1282129405235133632)
XLA Ops:
  0.6 0.0 copy-start.3
  0.6 0.0 copy-start.4
  0.7 0.0 copy-start.5
  0.7 0.0 copy-start.6
  0.7 0.0 copy-start.7
  0.7 0.0 copy-start.8
  0.7 1.6 %reshape.16 = bf16[8,352,128]{2,1,0:T(8,128)(2,1)S(1)} reshape(bf16[2,2,2,45056]{3,2,1,0:T(2,128)(2,1)} %param.10) | data formatting | bytes 1441792 | tf_op jit(solution)/shard_map/reshape | solution.py:419
  2.3 0.0 copy-start
  2.3 0.0 copy-start.1
  2.3 0.0 copy-start.2
  2.3 0.3 copy.12
  2.6 0.0 copy-done.3
  2.6 0.0 copy-done.4
  2.7 0.0 copy-done.5
  2.7 0.0 copy-done.6
  2.7 0.0 copy-done.7
  2.7 0.0 copy-done.8
  2.7 0.7 %copy-done = bf16[512,512]{1,0:T(8,128)(2,1)S(1)} copy-done((bf16[512,512]{1,0:T(8,128)(2,1)S(1)}, bf16[512,512]{1,0:T(8,128)(2,1)}, u32[]{:S(2)}) %copy-start) | copy-done | bytes 524312
  3.4 0.2 copy-done.1
  3.5 0.1 copy-done.2
  3.6 51.7 %shard_map.113 = (f32[128,256]{1,0:T(8,128)S(1)}, f32[64,176]{1,0:T(8,128)S(1)}) custom-call(bf16[176,16,128]{2,1,0:T(8,128)(2,1)S(1)} %bitcast.4, f32[12,4096]{1,0:T(8,128)S(1)} %copy-done.3, f32[12,256]{1,0:T(8,128)S(1)} %copy-done.7, f32[64,256]{1,0:T(8,128)S(1)} %copy-done.5, s32[16,128]{1,0:T(8,128)S(1)} %copy-done.8, bf16[128,128]{1,0:T(8,128)(2,1)S(1)} %copy-done.6, ...), custom_call_target="tpu_custom_call" | custom-call | tf_op jit(solution)/shard_map/pallas_call | solution.py:423
  55.3 0.7 %reshape.18 = f32[1,64,2,256]{3,2,1,0:T(2,128)} reshape(f32[128,256]{1,0:T(8,128)S(1)} %get-tuple-element.4) | data formatting | bytes 262144 | tf_op jit(solution)/shard_map/reshape | solution.py:472
  56.0 0.6 %copy.14 = f32[4,16,176]{2,1,0:T(8,128)} copy(f32[4,16,176]{2,1,0:T(8,128)S(1)} %bitcast.5) | data formatting | bytes 90112
Async XLA Ops:
  0.6 2.0 %copy-start.3 = (f32[12,4096]{1,0:T(8,128)S(1)}, f32[12,4096]{1,0:T(8,128)}, u32[]{:S(2)}) copy-start(f32[12,4096]{1,0:T(8,128)} %corr_taps.1) | copy-start | bytes 589828
  0.6 2.0 %copy-start.4 = (f32[2,64,256]{2,1,0:T(8,128)S(1)}, f32[2,64,256]{2,1,0:T(8,128)}, u32[]{:S(2)}) copy-start(f32[2,64,256]{2,1,0:T(8,128)} %constant.11.clone.twist) | copy-start | bytes 393220
  0.7 2.0 %copy-start.5 = (f32[64,256]{1,0:T(8,128)S(1)}, f32[64,256]{1,0:T(8,128)}, u32[]{:S(2)}) copy-start(f32[64,256]{1,0:T(8,128)} %angles.1) | copy-start | bytes 196612
  0.7 2.0 %copy-start.6 = (bf16[128,128]{1,0:T(8,128)(2,1)S(1)}, bf16[128,128]{1,0:T(8,128)(2,1)}, u32[]{:S(2)}) copy-start(bf16[128,128]{1,0:T(8,128)(2,1)} %constant.10.clone.first) | copy-start | bytes 98308
  0.7 2.0 %copy-start.7 = (f32[12,256]{1,0:T(8,128)S(1)}, f32[12,256]{1,0:T(8,128)}, u32[]{:S(2)}) copy-start(f32[12,256]{1,0:T(8,128)} %beam_taps.1) | copy-start | bytes 36868
  0.7 2.0 %copy-start.8 = (s32[16,128]{1,0:T(8,128)S(1)}, s32[16,128]{1,0:T(8,128)}, u32[]{:S(2)}) copy-start(s32[16,128]{1,0:T(8,128)} %index.1) | copy-start | bytes 24580
  2.3 1.0 %copy-start = (bf16[512,512]{1,0:T(8,128)(2,1)S(1)}, bf16[512,512]{1,0:T(8,128)(2,1)}, u32[]{:S(2)}) copy-start(bf16[512,512]{1,0:T(8,128)(2,1)} %constant.13.clone.short_hbm) | copy-start | bytes 1572868
  2.3 1.2 %copy-start.1 = (bf16[512,512]{1,0:T(8,128)(2,1)S(1)}, bf16[512,512]{1,0:T(8,128)(2,1)}, u32[]{:S(2)}) copy-start(bf16[512,512]{1,0:T(8,128)(2,1)} %constant.12.clone.second_hbm) | copy-start | bytes 1572868
  2.3 1.3 %copy-start.2 = (bf16[768,256]{1,0:T(8,128)(2,1)S(1)}, bf16[768,256]{1,0:T(8,128)(2,1)}, u32[]{:S(2)}) copy-start(bf16[768,256]{1,0:T(8,128)(2,1)} %constant.14.clone.pick_hbm) | copy-start | bytes 1179652

commit v5 on v4

--- a/solution.py
+++ b/solution.py
@@ -23,9 +23,9 @@
 HALF = 176
 FRAMES = 11
 SHORT_FRAMES = 176
-FRAMES_B = 48
+LATE = 40
 GROUPS = ((8, 3), (4, 4), (0, 4))
-FRAMES_A = SHORT_FRAMES - FRAMES_B
+BEAM_GROUPS = ((112, 64), (48, 64), (0, 48))
 
 
 def dft_tables(length):
@@ -98,10 +98,10 @@
     x_ref, corr_taps, beam_taps, angles, index, first, twist, second_hbm, short_hbm, pick_hbm,
     vis_ref, power_ref,
     second, short, pick,
-    hist, ext, fs, fl, z_ref, tw, send_a, recv_a, send_b, recv_b, send_spec, recv_spec,
+    hist, ext, fs, fl, z_ref, tw, send_beam, recv_beam, send_spec, recv_spec,
     table, weights, lhs, rhs, part_own, part_send, part_recv,
     row_sem, column_sem, table_sem, halo_send, halo_recv,
-    a_send_sem, a_recv_sem, b_send_sem, b_recv_sem, spec_send_sem, spec_recv_sem,
+    beam_send_sem, beam_recv_sem, spec_send_sem, spec_recv_sem, late_sem,
     part_send_sem, part_recv_sem,
 ):
     stn = lax.axis_index("stn")
@@ -150,8 +150,9 @@
                 fs[a, pl.ds(pl.multiple_of((i * step + f) * 8, 8), 8), :] = total
         return 0
 
-    def short_spectra(first_frame, frames, target):
-        lanes = target.shape[-1]
+    def short_spectra(c):
+        first_frame, frames = BEAM_GROUPS[c]
+        lax.fori_loop(first_frame // step, (first_frame + frames) // step, short_filter, 0)
         halves = []
         for st in range(2):
             for p in range(2):
@@ -160,16 +161,13 @@
                         z_ref[pl.ds(p * frames, frames), pl.ds(part * 256 + a * LANES, LANES)] = fs[
                             a, pl.ds(first_frame * 8 + part * 4 + st * 2 + p, frames, stride=8), :
                         ].astype(BF)
-            if lanes > 2 * frames:
-                z_ref[pl.ds(2 * frames, lanes - 2 * frames), :] = jnp.zeros(
-                    (lanes - 2 * frames, 512), BF
-                )
-            halves.append(dot_t(short[...], z_ref[pl.ds(0, lanes), :]).reshape(STN, 8, lanes))
-        target[...] = jnp.concatenate(halves, axis=1).astype(BF)
-
-    lax.fori_loop(FRAMES_B // step, SHORT_FRAMES // step, short_filter, 0)
+            if frames < 64:
+                z_ref[pl.ds(2 * frames, LANES - 2 * frames), :] = jnp.zeros((LANES - 2 * frames, 512), BF)
+            halves.append(dot_t(short[...], z_ref[...]).reshape(STN, 8, LANES))
+        send_beam[c] = jnp.concatenate(halves, axis=1).astype(BF)
+
     load(0).wait()
-    short_spectra(FRAMES_B, FRAMES_A, send_a)
+    short_spectra(0)
 
     @pl.when(grp == 0)
     def _():
@@ -196,11 +194,6 @@
             device_id_type=MESH,
         )
 
-    @pl.when(grp < GRP - 1)
-    def _():
-        for c in range(3):
-            halo(c).start()
-
     def exchange(source, target, send_sem, recv_sem, k):
         other = partner(stn, k)
         return pltpu.make_async_remote_copy(
@@ -229,17 +222,36 @@
         span = pl.ds(0, STN - 1)
         pltpu.make_async_copy(source.at[span], target.at[span], send_sem).wait()
 
-    a_args = (send_a, recv_a, a_send_sem, a_recv_sem)
-    b_args = (send_b, recv_b, b_send_sem, b_recv_sem)
+    beam_args = [
+        (send_beam.at[c], recv_beam.at[c], beam_send_sem.at[c], beam_recv_sem.at[c]) for c in range(3)
+    ]
     spec_args = [
         (send_spec.at[c], recv_spec.at[c], spec_send_sem.at[c], spec_recv_sem.at[c]) for c in range(3)
     ]
 
+    for k in range(4, STN // 2, 4):
+        exchange(*beam_args[0], k).start()
+    recv_beam[0, stn] = send_beam[0, stn]
+
+    @pl.when(grp < GRP - 1)
+    def _():
+        for c in range(3):
+            halo(c).start()
+
     pl.semaphore_wait(row_sem, 3)
     pl.semaphore_signal(column_sem, inc=1, device_id=(partner(stn, 32), grp), device_id_type=MESH)
-    send_all(*a_args, 1, STN // 2)
+
+    def to_plane(k, _):
+        exchange(*beam_args[0], k + 1 + k // 3).start()
+        return 0
+
+    lax.fori_loop(0, 24, to_plane, 0)
+    short_spectra(1)
+    send_all(*beam_args[1], 1, STN // 2)
+
     pl.semaphore_wait(column_sem, 1)
-    send_all(*a_args, STN // 2, STN)
+    send_all(*beam_args[0], STN // 2, STN)
+    send_all(*beam_args[1], STN // 2, STN)
 
     low = lax.broadcasted_iota(jnp.int32, (32, LANES), 1) < RADIX
     tw[FRAMES * RADIX : 12 * RADIX, :] = jnp.zeros((RADIX, 512), BF)
@@ -302,11 +314,13 @@
             for at in (first_frame * RADIX, first_frame * RADIX + LANES)
         ]
         send_spec[c] = jnp.concatenate(pairs, axis=1).astype(BF)
-        send_all(*spec_args[c])
-
-    lax.fori_loop(0, FRAMES_B // step, short_filter, 0)
-    short_spectra(0, FRAMES_B, send_b)
-    send_all(*b_args)
+        if c < 2:
+            send_all(*spec_args[c])
+        else:
+            send_all(*spec_args[c], 1, LATE)
+            send_all(send_spec.at[c], recv_spec.at[c], late_sem, spec_recv_sem.at[c], LATE, STN)
+
+    short_spectra(2)
 
     shape = (256, 1024)
     column = lax.broadcasted_iota(jnp.int32, shape, 1)
@@ -343,13 +357,15 @@
                 channel == ci, chosen_parts[po], 0.0
             ).astype(BF)
 
-    def beam_power(source):
-        fields = dot(weights[...], source[...].reshape(1024, source.shape[-1]))
-        return fields[:64] * fields[:64] + fields[64:] * fields[64:]
-
-    wait_all(*a_args)
-    power = beam_power(recv_a)
-    power_ref[:, FRAMES_B:SHORT_FRAMES] = power[:, :FRAMES_A] + power[:, FRAMES_A:]
+    def beam_power(c):
+        first_frame, frames = BEAM_GROUPS[c]
+        wait_all(*beam_args[c])
+        fields = dot(weights[...], recv_beam[c].reshape(1024, LANES))
+        power = fields[:64] * fields[:64] + fields[64:] * fields[64:]
+        power_ref[:, first_frame : first_frame + frames] = power[:, :frames] + power[:, frames : 2 * frames]
+
+    beam_power(0)
+    beam_power(1)
 
     def hand_over(k):
         other = lax.rem(grp + k, GRP)
@@ -364,6 +380,11 @@
 
     load(2).wait()
     for c in range(3):
+        if c == 2:
+            pltpu.make_async_copy(
+                send_spec.at[c, pl.ds(0, LATE - 1)], recv_spec.at[c, pl.ds(0, LATE - 1)], spec_send_sem.at[c]
+            ).wait()
+            send_all(*beam_args[2])
         wait_all(*spec_args[c])
 
         def gather_rows(b, _, c=c):
@@ -392,9 +413,7 @@
                 part_send[owner] = partial.astype(BF)
                 hand_over(k).start()
 
-    wait_all(*b_args)
-    power = beam_power(recv_b)
-    power_ref[:, 0:FRAMES_B] = power[:, :FRAMES_B] + power[:, FRAMES_B : 2 * FRAMES_B]
+    beam_power(2)
 
     total = part_own[0]
     for k in range(1, GRP):
@@ -404,10 +423,13 @@
 
     for k in range(1, GRP):
         hand_over(k).wait_send()
-    wait_sent(*a_args)
     for c in range(3):
+        wait_sent(*beam_args[c])
+    for c in range(2):
         wait_sent(*spec_args[c])
-    wait_sent(*b_args)
+    pltpu.make_async_copy(
+        send_spec.at[2, pl.ds(0, STN - LATE)], recv_spec.at[2, pl.ds(0, STN - LATE)], late_sem
+    ).wait()
 
     @pl.when(grp < GRP - 1)
     def _():
@@ -436,12 +458,10 @@
             pltpu.VMEM((2 * TILES, 8, LANES), F32),
             pltpu.VMEM((2, SHORT_FRAMES * 8, LANES), F32),
             pltpu.VMEM((FRAMES * 256, LANES), F32),
-            pltpu.VMEM((256, 512), BF),
+            pltpu.VMEM((LANES, 512), BF),
             pltpu.VMEM((12 * RADIX, 512), BF),
-            pltpu.VMEM((STN, 16, 256), BF),
-            pltpu.VMEM((STN, 16, 256), BF),
-            pltpu.VMEM((STN, 16, LANES), BF),
-            pltpu.VMEM((STN, 16, LANES), BF),
+            pltpu.VMEM((3, STN, 16, LANES), BF),
+            pltpu.VMEM((3, STN, 16, LANES), BF),
             pltpu.VMEM((3, STN, 16, LANES), BF),
             pltpu.VMEM((3, STN, 16, LANES), BF),
             pltpu.VMEM((2, 64, 1024), F32),
@@ -456,12 +476,11 @@
             dma((3,)),
             dma((3,)),
             dma((3,)),
+            dma((3,)),
+            dma((3,)),
+            dma((3,)),
+            dma((3,)),
             dma,
-            dma,
-            dma,
-            dma,
-            dma((3,)),
-            dma((3,)),
             dma((GRP - 1,)),
             dma((GRP - 1,)),
         ],

time: 56.8 us -> 55.5 us (0.977)
  Pallas kernels: 51.7 us -> 50.2 us
    pallas_call x1, Pallas kernels: 51.7 us -> 50.2 us  [on_device(): pl.pallas_call(kernel, out_shape=(jax.ShapeDtypeStruct((128, 256), F32),...]
where the time goes in v5:
time: 55.5 us; the launch traced here: 55.2 us
  Pallas kernels  50.2 us (90%)
  local copies, waits for them, and re-layouts  4.22 us (8%)
  between operations  0.77 us (1%)
    pallas_call x1, Pallas kernels, on_device(): pl.pallas_call(kernel, out_shape=(jax.ShapeDtypeStruct((128, 256), F32),...  50.2 us
    reshape x2, local copies, waits for them, and re-layouts, on_device(): voltages.reshape(8, TILES, LANES).transpose(1, 0, 2)  1.89 us
    unnamed x19, local copies, waits for them, and re-layouts  1.6 us

profile of v5, /device:TPU:1, one launch (start us, length us, event | category | flops | bytes accessed | tf_op | source)
XLA Modules:
  0.0 55.2 jit_solution(17762554865416818307)
XLA Ops:
  0.6 0.0 copy-start.3
  0.6 0.0 copy-start.4
  0.7 0.0 copy-start.5
  0.7 0.0 copy-start.6
  0.7 0.0 copy-start.7
  0.7 0.0 copy-start.8
  0.7 1.6 %reshape.16 = bf16[8,352,128]{2,1,0:T(8,128)(2,1)S(1)} reshape(bf16[2,2,2,45056]{3,2,1,0:T(2,128)(2,1)} %param.10) | data formatting | bytes 1441792 | tf_op jit(solution)/shard_map/reshape | solution.py:441
  2.3 0.0 copy-start
  2.3 0.0 copy-start.1
  2.3 0.0 copy-start.2
  2.3 0.3 copy.12
  2.6 0.0 copy-done.3
  2.6 0.0 copy-done.4
  2.7 0.0 copy-done.5
  2.7 0.0 copy-done.6
  2.7 0.0 copy-done.7
  2.7 0.0 copy-done.8
  2.7 0.7 %copy-done = bf16[512,512]{1,0:T(8,128)(2,1)S(1)} copy-done((bf16[512,512]{1,0:T(8,128)(2,1)S(1)}, bf16[512,512]{1,0:T(8,128)(2,1)}, u32[]{:S(2)}) %copy-start) | copy-done | bytes 524312
  3.4 0.2 copy-done.1
  3.5 0.1 copy-done.2
  3.6 50.2 %shard_map.113 = (f32[128,256]{1,0:T(8,128)S(1)}, f32[64,176]{1,0:T(8,128)S(1)}) custom-call(bf16[176,16,128]{2,1,0:T(8,128)(2,1)S(1)} %bitcast.4, f32[12,4096]{1,0:T(8,128)S(1)} %copy-done.3, f32[12,256]{1,0:T(8,128)S(1)} %copy-done.7, f32[64,256]{1,0:T(8,128)S(1)} %copy-done.5, s32[16,128]{1,0:T(8,128)S(1)} %copy-done.8, bf16[128,128]{1,0:T(8,128)(2,1)S(1)} %copy-done.6, ...), custom_call_target="tpu_custom_call" | custom-call | tf_op jit(solution)/shard_map/pallas_call | solution.py:445
  53.9 0.7 %reshape.18 = f32[1,64,2,256]{3,2,1,0:T(2,128)} reshape(f32[128,256]{1,0:T(8,128)S(1)} %get-tuple-element.4) | data formatting | bytes 262144 | tf_op jit(solution)/shard_map/reshape | solution.py:491
  54.6 0.6 %copy.14 = f32[4,16,176]{2,1,0:T(8,128)} copy(f32[4,16,176]{2,1,0:T(8,128)S(1)} %bitcast.5) | data formatting | bytes 90112
Async XLA Ops:
  0.6 2.0 %copy-start.3 = (f32[12,4096]{1,0:T(8,128)S(1)}, f32[12,4096]{1,0:T(8,128)}, u32[]{:S(2)}) copy-start(f32[12,4096]{1,0:T(8,128)} %corr_taps.1) | copy-start | bytes 589828
  0.6 2.0 %copy-start.4 = (f32[2,64,256]{2,1,0:T(8,128)S(1)}, f32[2,64,256]{2,1,0:T(8,128)}, u32[]{:S(2)}) copy-start(f32[2,64,256]{2,1,0:T(8,128)} %constant.11.clone.twist) | copy-start | bytes 393220
  0.7 2.0 %copy-start.5 = (f32[64,256]{1,0:T(8,128)S(1)}, f32[64,256]{1,0:T(8,128)}, u32[]{:S(2)}) copy-start(f32[64,256]{1,0:T(8,128)} %angles.1) | copy-start | bytes 196612
  0.7 2.0 %copy-start.6 = (bf16[128,128]{1,0:T(8,128)(2,1)S(1)}, bf16[128,128]{1,0:T(8,128)(2,1)}, u32[]{:S(2)}) copy-start(bf16[128,128]{1,0:T(8,128)(2,1)} %constant.10.clone.first) | copy-start | bytes 98308
  0.7 2.0 %copy-start.7 = (f32[12,256]{1,0:T(8,128)S(1)}, f32[12,256]{1,0:T(8,128)}, u32[]{:S(2)}) copy-start(f32[12,256]{1,0:T(8,128)} %beam_taps.1) | copy-start | bytes 36868
  0.7 2.0 %copy-start.8 = (s32[16,128]{1,0:T(8,128)S(1)}, s32[16,128]{1,0:T(8,128)}, u32[]{:S(2)}) copy-start(s32[16,128]{1,0:T(8,128)} %index.1) | copy-start | bytes 24580
  2.3 1.0 %copy-start = (bf16[512,512]{1,0:T(8,128)(2,1)S(1)}, bf16[512,512]{1,0:T(8,128)(2,1)}, u32[]{:S(2)}) copy-start(bf16[512,512]{1,0:T(8,128)(2,1)} %constant.13.clone.short_hbm) | copy-start | bytes 1572868
  2.3 1.2 %copy-start.1 = (bf16[512,512]{1,0:T(8,128)(2,1)S(1)}, bf16[512,512]{1,0:T(8,128)(2,1)}, u32[]{:S(2)}) copy-start(bf16[512,512]{1,0:T(8,128)(2,1)} %constant.12.clone.second_hbm) | copy-start | bytes 1572868
  2.3 1.3 %copy-start.2 = (bf16[768,256]{1,0:T(8,128)(2,1)S(1)}, bf16[768,256]{1,0:T(8,128)(2,1)}, u32[]{:S(2)}) copy-start(bf16[768,256]{1,0:T(8,128)(2,1)} %constant.14.clone.pick_hbm) | copy-start | bytes 1179652

commit v6 on v5

--- a/solution.py
+++ b/solution.py
@@ -69,6 +69,7 @@
                 pick[pair, 128 + 2 * u + 1, src, pair, q, 0] = -1
                 pick[pair, 256 + u, src, pair, q, 0] = 1
                 pick[pair, 320 + u, src, pair, q, 1] = 1
+    pick_half = pick[0, :, :, 0].reshape(384, 128)
     pick = pick.reshape(768, 256)
     return (
         first.astype(bf),
@@ -76,6 +77,7 @@
         second.astype(bf),
         short.astype(bf),
         pick.astype(bf),
+        pick_half.astype(bf),
     )
 
 
@@ -95,13 +97,13 @@
 
 
 def kernel(
-    x_ref, corr_taps, beam_taps, angles, index, first, twist, second_hbm, short_hbm, pick_hbm,
+    x_ref, corr_taps, beam_taps, angles, index, first, twist, second_hbm, short_hbm, pick_hbm, pick_half_hbm,
     vis_ref, power_ref,
-    second, short, pick,
-    hist, ext, fs, fl, z_ref, tw, send_beam, recv_beam, send_spec, recv_spec,
+    second, short, pick, pick_half,
+    hist, ext, fs, fl, z_ref, tw, tail_tw, send_beam, recv_beam, send_spec, recv_spec, send_half, recv_half,
     table, weights, lhs, rhs, part_own, part_send, part_recv,
     row_sem, column_sem, table_sem, halo_send, halo_recv,
-    beam_send_sem, beam_recv_sem, spec_send_sem, spec_recv_sem, late_sem,
+    beam_send_sem, beam_recv_sem, spec_send_sem, spec_recv_sem, half_send_sem, half_recv_sem, late_sem,
     part_send_sem, part_recv_sem,
 ):
     stn = lax.axis_index("stn")
@@ -119,10 +121,10 @@
         )
 
     def load(i):
-        source, target = ((short_hbm, short), (second_hbm, second), (pick_hbm, pick))[i]
+        source, target = ((short_hbm, short), (second_hbm, second), (pick_hbm, pick), (pick_half_hbm, pick_half))[i]
         return pltpu.make_async_copy(source, target, table_sem.at[i])
 
-    for i in range(3):
+    for i in range(4):
         load(i).start()
 
     def widen_own(i, _):
@@ -150,7 +152,7 @@
                 fs[a, pl.ds(pl.multiple_of((i * step + f) * 8, 8), 8), :] = total
         return 0
 
-    def short_spectra(c):
+    def short_spectra(c, beside=None):
         first_frame, frames = BEAM_GROUPS[c]
         lax.fori_loop(first_frame // step, (first_frame + frames) // step, short_filter, 0)
         halves = []
@@ -164,7 +166,10 @@
             if frames < 64:
                 z_ref[pl.ds(2 * frames, LANES - 2 * frames), :] = jnp.zeros((LANES - 2 * frames, 512), BF)
             halves.append(dot_t(short[...], z_ref[...]).reshape(STN, 8, LANES))
-        send_beam[c] = jnp.concatenate(halves, axis=1).astype(BF)
+        block = jnp.concatenate(halves, axis=1)
+        if beside is not None:
+            block = block + beside
+        send_beam[c] = block.astype(BF)
 
     load(0).wait()
     short_spectra(0)
@@ -226,8 +231,9 @@
         (send_beam.at[c], recv_beam.at[c], beam_send_sem.at[c], beam_recv_sem.at[c]) for c in range(3)
     ]
     spec_args = [
-        (send_spec.at[c], recv_spec.at[c], spec_send_sem.at[c], spec_recv_sem.at[c]) for c in range(3)
+        (send_spec.at[c], recv_spec.at[c], spec_send_sem.at[c], spec_recv_sem.at[c]) for c in range(2)
     ]
+    half_args = (send_half, recv_half, half_send_sem, half_recv_sem)
 
     for k in range(4, STN // 2, 4):
         exchange(*beam_args[0], k).start()
@@ -251,10 +257,9 @@
 
     pl.semaphore_wait(column_sem, 1)
     send_all(*beam_args[0], STN // 2, STN)
-    send_all(*beam_args[1], STN // 2, STN)
 
     low = lax.broadcasted_iota(jnp.int32, (32, LANES), 1) < RADIX
-    tw[FRAMES * RADIX : 12 * RADIX, :] = jnp.zeros((RADIX, 512), BF)
+    tail_tw[...] = jnp.zeros((2 * LANES, 512), BF)
 
     for c, (first_frame, frames) in enumerate(GROUPS):
 
@@ -307,20 +312,29 @@
 
         lax.fori_loop(first_frame, first_frame + frames, first_factor, 0)
 
+        def second_factor(rows):
+            return dot_t(second[...], rows).reshape(STN, 8, LANES)
+
         if c == 0:
             load(1).wait()
-        pairs = [
-            dot_t(second[...], tw[at : at + LANES, :]).reshape(STN, 8, LANES)
-            for at in (first_frame * RADIX, first_frame * RADIX + LANES)
-        ]
-        send_spec[c] = jnp.concatenate(pairs, axis=1).astype(BF)
-        if c < 2:
-            send_all(*spec_args[c])
+            send_half[...] = second_factor(tw[8 * RADIX : 10 * RADIX, :]).astype(BF)
+            send_all(*half_args)
+            tail_tw[96:128, :] = tw[640:672, :]
+            tail_tw[224:256, :] = tw[672:704, :]
+            tail = [second_factor(tail_tw[e * LANES : (e + 1) * LANES, :]) for e in range(2)]
+            short_spectra(2, jnp.concatenate(tail, axis=1))
+            send_all(*beam_args[2])
         else:
-            send_all(*spec_args[c], 1, LATE)
-            send_all(send_spec.at[c], recv_spec.at[c], late_sem, spec_recv_sem.at[c], LATE, STN)
-
-    short_spectra(2)
+            pairs = [
+                second_factor(tw[at : at + LANES, :])
+                for at in (first_frame * RADIX, first_frame * RADIX + LANES)
+            ]
+            send_spec[c - 1] = jnp.concatenate(pairs, axis=1).astype(BF)
+            if c == 1:
+                send_all(*spec_args[0])
+            else:
+                send_all(*spec_args[1], 1, LATE)
+                send_all(send_spec.at[1], recv_spec.at[1], late_sem, spec_recv_sem.at[1], LATE, STN)
 
     shape = (256, 1024)
     column = lax.broadcasted_iota(jnp.int32, shape, 1)
@@ -365,7 +379,6 @@
         power_ref[:, first_frame : first_frame + frames] = power[:, :frames] + power[:, frames : 2 * frames]
 
     beam_power(0)
-    beam_power(1)
 
     def hand_over(k):
         other = lax.rem(grp + k, GRP)
@@ -378,21 +391,18 @@
             device_id_type=MESH,
         )
 
-    load(2).wait()
-    for c in range(3):
-        if c == 2:
-            pltpu.make_async_copy(
-                send_spec.at[c, pl.ds(0, LATE - 1)], recv_spec.at[c, pl.ds(0, LATE - 1)], spec_send_sem.at[c]
-            ).wait()
-            send_all(*beam_args[2])
-        wait_all(*spec_args[c])
-
-        def gather_rows(b, _, c=c):
-            block = recv_spec[c, pl.ds(b * 16, 16)].reshape(256, LANES)
-            rows = dot(pick[...], block).astype(BF)
+    def correlate(source, selection, pairs, masked, first_block, last_block):
+        rows_each = source.shape[1]
+
+        def gather_rows(b, _):
+            block = source[pl.ds(b * 16, 16)].reshape(16 * rows_each, LANES)
+            rows = dot(selection[...], block)
+            if masked:
+                rows = jnp.where(lax.broadcasted_iota(jnp.int32, rows.shape, 1) >= 96, rows, 0.0)
+            rows = rows.astype(BF)
             wide = pl.ds(pl.multiple_of(b * 128, 128), 128)
             narrow = pl.ds(pl.multiple_of(b * 64, 64), 64)
-            for e in range(2):
+            for e in range(pairs):
                 at = 384 * e
                 lanes = 2 * e * LANES
                 lhs[wide, lanes : lanes + LANES] = rows[at : at + 128]
@@ -402,18 +412,34 @@
             return 0
 
         lax.fori_loop(0, 4, gather_rows, 0)
+        depth = 2 * pairs * LANES
         for k in (1, 2, 3, 0):
             owner = lax.rem(grp + k, GRP)
-            partial = dot_t(lhs[pl.ds(pl.multiple_of(owner * 128, 128), 128), :], rhs[...])
-            if c > 0:
+            partial = dot_t(lhs[pl.ds(pl.multiple_of(owner * 128, 128), 128), 0:depth], rhs[:, 0:depth])
+            if not first_block:
                 partial = partial + part_own[k]
-            if c < 2 or k == 0:
+            if not last_block or k == 0:
                 part_own[k] = partial
             else:
                 part_send[owner] = partial.astype(BF)
                 hand_over(k).start()
 
+    load(2).wait()
+    load(3).wait()
+    wait_all(*half_args)
+    correlate(recv_half, pick_half, 1, False, True, False)
     beam_power(2)
+    correlate(recv_beam.at[2], pick, 2, True, False, False)
+    wait_all(*spec_args[0])
+    correlate(recv_spec.at[0], pick, 2, False, False, False)
+    pltpu.make_async_copy(
+        send_spec.at[1, pl.ds(0, LATE - 1)], recv_spec.at[1, pl.ds(0, LATE - 1)], spec_send_sem.at[1]
+    ).wait()
+    send_all(*beam_args[1], STN // 2, STN)
+    wait_all(*spec_args[1])
+    correlate(recv_spec.at[1], pick, 2, False, False, True)
+
+    beam_power(1)
 
     total = part_own[0]
     for k in range(1, GRP):
@@ -425,10 +451,10 @@
         hand_over(k).wait_send()
     for c in range(3):
         wait_sent(*beam_args[c])
-    for c in range(2):
-        wait_sent(*spec_args[c])
+    wait_sent(*half_args)
+    wait_sent(*spec_args[0])
     pltpu.make_async_copy(
-        send_spec.at[2, pl.ds(0, STN - LATE)], recv_spec.at[2, pl.ds(0, STN - LATE)], late_sem
+        send_spec.at[1, pl.ds(0, STN - LATE)], recv_spec.at[1, pl.ds(0, STN - LATE)], late_sem
     ).wait()
 
     @pl.when(grp < GRP - 1)
@@ -448,22 +474,26 @@
             jax.ShapeDtypeStruct((128, 256), F32),
             jax.ShapeDtypeStruct((64, SHORT_FRAMES), F32),
         ),
-        in_specs=[vmem] * 7 + [pl.BlockSpec(memory_space=pltpu.HBM)] * 3,
+        in_specs=[vmem] * 7 + [pl.BlockSpec(memory_space=pltpu.HBM)] * 4,
         out_specs=(vmem, vmem),
         scratch_shapes=[
             pltpu.VMEM((512, 512), BF),
             pltpu.VMEM((512, 512), BF),
             pltpu.VMEM((768, 256), BF),
+            pltpu.VMEM((384, LANES), BF),
             pltpu.VMEM((HALF, 16, LANES), BF),
             pltpu.VMEM((2 * TILES, 8, LANES), F32),
             pltpu.VMEM((2, SHORT_FRAMES * 8, LANES), F32),
             pltpu.VMEM((FRAMES * 256, LANES), F32),
             pltpu.VMEM((LANES, 512), BF),
-            pltpu.VMEM((12 * RADIX, 512), BF),
+            pltpu.VMEM((FRAMES * RADIX, 512), BF),
+            pltpu.VMEM((2 * LANES, 512), BF),
             pltpu.VMEM((3, STN, 16, LANES), BF),
             pltpu.VMEM((3, STN, 16, LANES), BF),
-            pltpu.VMEM((3, STN, 16, LANES), BF),
-            pltpu.VMEM((3, STN, 16, LANES), BF),
+            pltpu.VMEM((2, STN, 16, LANES), BF),
+            pltpu.VMEM((2, STN, 16, LANES), BF),
+            pltpu.VMEM((STN, 8, LANES), BF),
+            pltpu.VMEM((STN, 8, LANES), BF),
             pltpu.VMEM((2, 64, 1024), F32),
             pltpu.VMEM((128, 1024), BF),
             pltpu.VMEM((512, 512), BF),
@@ -473,13 +503,15 @@
             pltpu.VMEM((GRP - 1, 128, 256), BF),
             pltpu.SemaphoreType.REGULAR,
             pltpu.SemaphoreType.REGULAR,
+            dma((4,)),
             dma((3,)),
             dma((3,)),
             dma((3,)),
             dma((3,)),
-            dma((3,)),
-            dma((3,)),
-            dma((3,)),
+            dma((2,)),
+            dma((2,)),
+            dma,
+            dma,
             dma,
             dma((GRP - 1,)),
             dma((GRP - 1,)),

time: 55.5 us -> 54.7 us (0.986)
  Pallas kernels: 50.2 us -> 49.5 us
    pallas_call x1, Pallas kernels: 50.2 us -> 49.5 us  [on_device(): pl.pallas_call(kernel, out_shape=(jax.ShapeDtypeStruct((128, 256), F32),...]
    unnamed x19 -> x21, local copies, waits for them, and re-layouts: 1.6 us -> 1.6 us
where the time goes in v6:
time: 54.7 us; the launch traced here: 54.5 us
  Pallas kernels  49.5 us (90%)
  local copies, waits for them, and re-layouts  4.23 us (8%)
  between operations  0.79 us (1%)
    pallas_call x1, Pallas kernels, on_device(): pl.pallas_call(kernel, out_shape=(jax.ShapeDtypeStruct((128, 256), F32),...  49.5 us
    reshape x2, local copies, waits for them, and re-layouts, on_device(): voltages.reshape(8, TILES, LANES).transpose(1, 0, 2)  1.9 us
    unnamed x21, local copies, waits for them, and re-layouts  1.6 us

profile of v6, /device:TPU:1, one launch (start us, length us, event | category | flops | bytes accessed | tf_op | source)
XLA Modules:
  0.0 54.5 jit_solution(15502578795250094869)
XLA Ops:
  0.6 0.0 copy-start.3
  0.6 0.0 copy-start.4
  0.7 0.0 copy-start.5
  0.7 0.0 copy-start.6
  0.7 0.0 copy-start.7
  0.7 0.0 copy-start.8
  0.7 0.0 copy-start.9
  0.7 1.6 %reshape.16 = bf16[8,352,128]{2,1,0:T(8,128)(2,1)S(1)} reshape(bf16[2,2,2,45056]{3,2,1,0:T(2,128)(2,1)} %param.11) | data formatting | bytes 1441792 | tf_op jit(solution)/shard_map/reshape | solution.py:467
  2.3 0.0 copy-start
  2.3 0.0 copy-start.1
  2.4 0.0 copy-start.2
  2.4 0.3 copy.13
  2.7 0.0 copy-done.3
  2.7 0.0 copy-done.4
  2.7 0.0 copy-done.5
  2.7 0.0 copy-done.6
  2.7 0.0 copy-done.7
  2.7 0.0 copy-done.8
  2.7 0.6 %copy-done = bf16[512,512]{1,0:T(8,128)(2,1)S(1)} copy-done((bf16[512,512]{1,0:T(8,128)(2,1)S(1)}, bf16[512,512]{1,0:T(8,128)(2,1)}, u32[]{:S(2)}) %copy-start) | copy-done | bytes 524312
  3.4 0.2 copy-done.1
  3.5 0.1 copy-done.2
  3.7 49.5 %shard_map.122 = (f32[128,256]{1,0:T(8,128)S(1)}, f32[64,176]{1,0:T(8,128)S(1)}) custom-call(bf16[176,16,128]{2,1,0:T(8,128)(2,1)S(1)} %bitcast.4, f32[12,4096]{1,0:T(8,128)S(1)} %copy-done.3, f32[12,256]{1,0:T(8,128)S(1)} %copy-done.8, f32[64,256]{1,0:T(8,128)S(1)} %copy-done.6, s32[16,128]{1,0:T(8,128)S(1)} %copy-done.9, bf16[128,128]{1,0:T(8,128)(2,1)S(1)} %copy-done.7, ...), custom_call_target="tpu_custom_call" | custom-call | tf_op jit(solution)/shard_map/pallas_call | solution.py:471
  53.2 0.7 %reshape.18 = f32[1,64,2,256]{3,2,1,0:T(2,128)} reshape(f32[128,256]{1,0:T(8,128)S(1)} %get-tuple-element.4) | data formatting | bytes 262144 | tf_op jit(solution)/shard_map/reshape | solution.py:523
  53.9 0.6 %copy.15 = f32[4,16,176]{2,1,0:T(8,128)} copy(f32[4,16,176]{2,1,0:T(8,128)S(1)} %bitcast.5) | data formatting | bytes 90112
  (1 shorter events, 0.0 us)
Async XLA Ops:
  0.6 2.0 %copy-start.3 = (f32[12,4096]{1,0:T(8,128)S(1)}, f32[12,4096]{1,0:T(8,128)}, u32[]{:S(2)}) copy-start(f32[12,4096]{1,0:T(8,128)} %corr_taps.1) | copy-start | bytes 589828
  0.6 2.0 %copy-start.4 = (f32[2,64,256]{2,1,0:T(8,128)S(1)}, f32[2,64,256]{2,1,0:T(8,128)}, u32[]{:S(2)}) copy-start(f32[2,64,256]{2,1,0:T(8,128)} %constant.13.clone.twist) | copy-start | bytes 393220
  0.7 2.0 %copy-start.5 = (bf16[384,128]{1,0:T(8,128)(2,1)S(1)}, bf16[384,128]{1,0:T(8,128)(2,1)}, u32[]{:S(2)}) copy-start(bf16[384,128]{1,0:T(8,128)(2,1)} %constant.17.clone.pick_half_hbm) | copy-start | bytes 294916
  0.7 2.0 %copy-start.6 = (f32[64,256]{1,0:T(8,128)S(1)}, f32[64,256]{1,0:T(8,128)}, u32[]{:S(2)}) copy-start(f32[64,256]{1,0:T(8,128)} %angles.1) | copy-start | bytes 196612
  0.7 2.0 %copy-start.7 = (bf16[128,128]{1,0:T(8,128)(2,1)S(1)}, bf16[128,128]{1,0:T(8,128)(2,1)}, u32[]{:S(2)}) copy-start(bf16[128,128]{1,0:T(8,128)(2,1)} %constant.12.clone.first) | copy-start | bytes 98308
  0.7 2.0 %copy-start.8 = (f32[12,256]{1,0:T(8,128)S(1)}, f32[12,256]{1,0:T(8,128)}, u32[]{:S(2)}) copy-start(f32[12,256]{1,0:T(8,128)} %beam_taps.1) | copy-start | bytes 36868
  0.7 2.0 %copy-start.9 = (s32[16,128]{1,0:T(8,128)S(1)}, s32[16,128]{1,0:T(8,128)}, u32[]{:S(2)}) copy-start(s32[16,128]{1,0:T(8,128)} %index.1) | copy-start | bytes 24580
  2.3 1.0 %copy-start = (bf16[512,512]{1,0:T(8,128)(2,1)S(1)}, bf16[512,512]{1,0:T(8,128)(2,1)}, u32[]{:S(2)}) copy-start(bf16[512,512]{1,0:T(8,128)(2,1)} %constant.15.clone.short_hbm) | copy-start | bytes 1572868
  2.3 1.2 %copy-start.1 = (bf16[512,512]{1,0:T(8,128)(2,1)S(1)}, bf16[512,512]{1,0:T(8,128)(2,1)}, u32[]{:S(2)}) copy-start(bf16[512,512]{1,0:T(8,128)(2,1)} %constant.14.clone.second_hbm) | copy-start | bytes 1572868
  2.4 1.3 %copy-start.2 = (bf16[768,256]{1,0:T(8,128)(2,1)S(1)}, bf16[768,256]{1,0:T(8,128)(2,1)}, u32[]{:S(2)}) copy-start(bf16[768,256]{1,0:T(8,128)(2,1)} %constant.16.clone.pick_hbm) | copy-start | bytes 1179652

commit v7 on v6

--- a/solution.py
+++ b/solution.py
@@ -23,7 +23,7 @@
 HALF = 176
 FRAMES = 11
 SHORT_FRAMES = 176
-LATE = 40
+LATE = 16
 GROUPS = ((8, 3), (4, 4), (0, 4))
 BEAM_GROUPS = ((112, 64), (48, 64), (0, 48))
 
@@ -97,10 +97,11 @@
 
 
 def kernel(
-    x_ref, corr_taps, beam_taps, angles, index, first, twist, second_hbm, short_hbm, pick_hbm, pick_half_hbm,
+    volts_hbm, corr_taps_hbm, beam_taps_hbm, angles_hbm, index_hbm, first_hbm, twist_hbm, second_hbm,
+    short_hbm, pick_hbm, pick_half_hbm,
     vis_ref, power_ref,
-    second, short, pick, pick_half,
-    hist, ext, fs, fl, z_ref, tw, tail_tw, send_beam, recv_beam, send_spec, recv_spec, send_half, recv_half,
+    second, short, pick, pick_half, volts, corr_taps, beam_taps, angles, index, first, twist,
+    x_ref, hist, ext, fs, fl, z_ref, tw, tail_tw, send_beam, recv_beam, send_spec, recv_spec, send_half, recv_half,
     table, weights, lhs, rhs, part_own, part_send, part_recv,
     row_sem, column_sem, table_sem, halo_send, halo_recv,
     beam_send_sem, beam_recv_sem, spec_send_sem, spec_recv_sem, half_send_sem, half_recv_sem, late_sem,
@@ -121,18 +122,35 @@
         )
 
     def load(i):
-        source, target = ((short_hbm, short), (second_hbm, second), (pick_hbm, pick), (pick_half_hbm, pick_half))[i]
+        source, target = (
+            (volts_hbm, volts),
+            (beam_taps_hbm, beam_taps),
+            (short_hbm, short),
+            (corr_taps_hbm, corr_taps),
+            (first_hbm, first),
+            (twist_hbm, twist),
+            (second_hbm, second),
+            (angles_hbm, angles),
+            (index_hbm, index),
+            (pick_hbm, pick),
+            (pick_half_hbm, pick_half),
+        )[i]
         return pltpu.make_async_copy(source, target, table_sem.at[i])
 
-    for i in range(4):
+    for i in range(11):
         load(i).start()
 
     def widen_own(i, _):
-        v = x_ref[i].astype(F32)
-        ext[TILES + 2 * i] = v[:8]
-        ext[TILES + 2 * i + 1] = v[8:]
+        both = []
+        for e in range(2):
+            at = pl.ds(pl.multiple_of((2 * i + e) * LANES, LANES), LANES)
+            v = jnp.concatenate([volts[j, :, at].astype(F32) for j in range(4)], axis=0)
+            ext[TILES + 2 * i + e] = v
+            both.append(v)
+        x_ref[i] = jnp.concatenate(both, axis=0).astype(BF)
         return 0
 
+    load(0).wait()
     lax.fori_loop(0, HALF, widen_own, 0, unroll=8)
 
     step = 8
@@ -171,7 +189,8 @@
             block = block + beside
         send_beam[c] = block.astype(BF)
 
-    load(0).wait()
+    load(1).wait()
+    load(2).wait()
     short_spectra(0)
 
     @pl.when(grp == 0)
@@ -258,6 +277,8 @@
     pl.semaphore_wait(column_sem, 1)
     send_all(*beam_args[0], STN // 2, STN)
 
+    for i in range(3, 11):
+        load(i).wait()
     low = lax.broadcasted_iota(jnp.int32, (32, LANES), 1) < RADIX
     tail_tw[...] = jnp.zeros((2 * LANES, 512), BF)
 
@@ -316,7 +337,6 @@
             return dot_t(second[...], rows).reshape(STN, 8, LANES)
 
         if c == 0:
-            load(1).wait()
             send_half[...] = second_factor(tw[8 * RADIX : 10 * RADIX, :]).astype(BF)
             send_all(*half_args)
             tail_tw[96:128, :] = tw[640:672, :]
@@ -424,8 +444,6 @@
                 part_send[owner] = partial.astype(BF)
                 hand_over(k).start()
 
-    load(2).wait()
-    load(3).wait()
     wait_all(*half_args)
     correlate(recv_half, pick_half, 1, False, True, False)
     beam_power(2)
@@ -445,7 +463,9 @@
     for k in range(1, GRP):
         hand_over(k).wait_recv()
         total = total + part_recv[k - 1].astype(F32)
-    vis_ref[...] = total * (1.0 / math.sqrt(4 * FRAMES * RADIX))
+    total = total * (1.0 / math.sqrt(4 * FRAMES * RADIX))
+    for u in range(64):
+        vis_ref[0, u] = total[2 * u : 2 * u + 2]
 
     for k in range(1, GRP):
         hand_over(k).wait_send()
@@ -464,23 +484,31 @@
 
 
 def on_device(voltages, corr_taps, beam_taps, angle_table, table_index):
-    x = voltages.reshape(8, TILES, LANES).transpose(1, 0, 2).reshape(HALF, 16, LANES)
+    volts = voltages.reshape(4, 2, TILES * LANES)
     tables = [jnp.asarray(t) for t in constant_tables()]
     vmem = pl.BlockSpec(memory_space=pltpu.VMEM)
     dma = pltpu.SemaphoreType.DMA
     vis, power = pl.pallas_call(
         kernel,
         out_shape=(
-            jax.ShapeDtypeStruct((128, 256), F32),
+            jax.ShapeDtypeStruct((1, 64, 2, 256), F32),
             jax.ShapeDtypeStruct((64, SHORT_FRAMES), F32),
         ),
-        in_specs=[vmem] * 7 + [pl.BlockSpec(memory_space=pltpu.HBM)] * 4,
+        in_specs=[pl.BlockSpec(memory_space=pl.ANY)] * 11,
         out_specs=(vmem, vmem),
         scratch_shapes=[
             pltpu.VMEM((512, 512), BF),
             pltpu.VMEM((512, 512), BF),
             pltpu.VMEM((768, 256), BF),
             pltpu.VMEM((384, LANES), BF),
+            pltpu.VMEM((4, 2, TILES * LANES), BF),
+            pltpu.VMEM((TAPS, RADIX * RADIX), F32),
+            pltpu.VMEM((TAPS, 256), F32),
+            pltpu.VMEM((64, 256), F32),
+            pltpu.VMEM((16, 128), jnp.int32),
+            pltpu.VMEM((128, 128), BF),
+            pltpu.VMEM((2, 64, 256), F32),
+            pltpu.VMEM((HALF, 16, LANES), BF),
             pltpu.VMEM((HALF, 16, LANES), BF),
             pltpu.VMEM((2 * TILES, 8, LANES), F32),
             pltpu.VMEM((2, SHORT_FRAMES * 8, LANES), F32),
@@ -503,7 +531,7 @@
             pltpu.VMEM((GRP - 1, 128, 256), BF),
             pltpu.SemaphoreType.REGULAR,
             pltpu.SemaphoreType.REGULAR,
-            dma((4,)),
+            dma((11,)),
             dma((3,)),
             dma((3,)),
             dma((3,)),
@@ -517,10 +545,10 @@
             dma((GRP - 1,)),
         ],
         compiler_params=pltpu.CompilerParams(
-            collective_id=0, has_side_effects=True, vmem_limit_bytes=48 * 1024 * 1024
+            collective_id=0, has_side_effects=True, vmem_limit_bytes=60 * 1024 * 1024
         ),
-    )(x, corr_taps, beam_taps, angle_table, table_index, *tables)
-    return vis.reshape(1, 64, 2, 256), power.reshape(4, 16, SHORT_FRAMES)
+    )(volts, corr_taps, beam_taps, angle_table, table_index, *tables)
+    return vis, power.reshape(4, 16, SHORT_FRAMES)
 
 
 def solution(mesh):

time: 54.7 us -> 54.4 us (level)
  local copies, waits for them, and re-layouts: 4.23 us -> 2.23 us
  Pallas kernels: 49.5 us -> 51.4 us
    reshape x3 -> x0, local copies, waits for them, and re-layouts: 2.63 us -> none  [the longest x2 1.9 us: on_device(): voltages.reshape(8, TILES, LANES).transpose(1, 0, 2)]
    pallas_call x1, Pallas kernels: 49.5 us -> 51.4 us  [on_device(): pl.pallas_call(kernel, out_shape=(jax.ShapeDtypeStruct((1, 64, 2, 256), F...]
    unnamed x21 -> x4, local copies, waits for them, and re-layouts: 1.6 us -> 2.23 us
where the time goes in v7:
time: 54.4 us; the launch traced here: 54.3 us
  Pallas kernels  51.4 us (94%)
  local copies, waits for them, and re-layouts  2.23 us (4%)
  between operations  0.65 us (1%)
    pallas_call x1, Pallas kernels, on_device(): pl.pallas_call(kernel, out_shape=(jax.ShapeDtypeStruct((1, 64, 2, 256), F...  51.4 us
    unnamed x4, local copies, waits for them, and re-layouts  2.23 us

profile of v7, /device:TPU:1, one launch (start us, length us, event | category | flops | bytes accessed | tf_op | source)
XLA Modules:
  0.0 54.3 jit_solution(13178507438942561098)
XLA Ops:
  0.6 51.4 %shard_map.122 = (f32[1,64,2,256]{3,2,1,0:T(2,128)}, f32[64,176]{1,0:T(8,128)}) custom-call(bf16[4,2,45056]{2,1,0:T(2,128)(2,1)} %bitcast.2, f32[12,4096]{1,0:T(8,128)} %corr_taps_hbm.1, f32[12,256]{1,0:T(8,128)} %beam_taps_hbm.1, f32[64,256]{1,0:T(8,128)} %angles_hbm.1, s32[16,128]{1,0:T(8,128)} %index_hbm.1, bf16[128,128]{1,0:T(8,128)(2,1)} %constant.12.clone.first_hbm, ...), custom_call_target="tpu_custom_call" | custom-call | tf_op jit(solution)/shard_map/pallas_call | solution.py:491
  52.1 0.0 copy-start
  52.1 1.6 %copy.15 = f32[1,64,2,256]{3,2,1,0:T(2,128)} copy(f32[1,64,2,256]{3,2,1,0:T(2,128)} %get-tuple-element.8) | data formatting | bytes 262144
  53.7 0.0 copy-done
  53.7 0.6 %copy.16 = f32[4,16,176]{2,1,0:T(8,128)} copy(f32[4,16,176]{2,1,0:T(8,128)S(1)} %bitcast.3) | data formatting | bytes 90112
Async XLA Ops:
  52.1 1.6 %copy-start = (f32[64,176]{1,0:T(8,128)S(1)}, f32[64,176]{1,0:T(8,128)}, u32[]{:S(2)}) copy-start(f32[64,176]{1,0:T(8,128)} %get-tuple-element.5) | copy-start | bytes 135172

commit v8 on v7

--- a/solution.py
+++ b/solution.py
@@ -151,7 +151,7 @@
         return 0
 
     load(0).wait()
-    lax.fori_loop(0, HALF, widen_own, 0, unroll=8)
+    lax.fori_loop(96, HALF, widen_own, 0, unroll=8)
 
     step = 8
 
@@ -260,8 +260,7 @@
 
     @pl.when(grp < GRP - 1)
     def _():
-        for c in range(3):
-            halo(c).start()
+        halo(0).start()
 
     pl.semaphore_wait(row_sem, 3)
     pl.semaphore_signal(column_sem, inc=1, device_id=(partner(stn, 32), grp), device_id_type=MESH)
@@ -271,6 +270,13 @@
         return 0
 
     lax.fori_loop(0, 24, to_plane, 0)
+    lax.fori_loop(0, 96, widen_own, 0, unroll=8)
+
+    @pl.when(grp < GRP - 1)
+    def _():
+        halo(1).start()
+        halo(2).start()
+
     short_spectra(1)
     send_all(*beam_args[1], 1, STN // 2)
 

time: 54.4 us -> 54 us (level)
  no operation moved by 1% of the time
where the time goes in v8:
time: 54 us; the launch traced here: 53.9 us
  Pallas kernels  51 us (94%)
  local copies, waits for them, and re-layouts  2.23 us (4%)
  between operations  0.65 us (1%)
    pallas_call x1, Pallas kernels, on_device(): pl.pallas_call(kernel, out_shape=(jax.ShapeDtypeStruct((1, 64, 2, 256), F...  51 us
    unnamed x4, local copies, waits for them, and re-layouts  2.23 us

profile of v8, /device:TPU:1, one launch (start us, length us, event | category | flops | bytes accessed | tf_op | source)
XLA Modules:
  0.0 53.9 jit_solution(6559133728273040115)
XLA Ops:
  0.6 51.0 %shard_map.122 = (f32[1,64,2,256]{3,2,1,0:T(2,128)}, f32[64,176]{1,0:T(8,128)}) custom-call(bf16[4,2,45056]{2,1,0:T(2,128)(2,1)} %bitcast.2, f32[12,4096]{1,0:T(8,128)} %corr_taps_hbm.1, f32[12,256]{1,0:T(8,128)} %beam_taps_hbm.1, f32[64,256]{1,0:T(8,128)} %angles_hbm.1, s32[16,128]{1,0:T(8,128)} %index_hbm.1, bf16[128,128]{1,0:T(8,128)(2,1)} %constant.12.clone.first_hbm, ...), custom_call_target="tpu_custom_call" | custom-call | tf_op jit(solution)/shard_map/pallas_call | solution.py:497
  51.7 0.0 copy-start
  51.7 1.6 %copy.15 = f32[1,64,2,256]{3,2,1,0:T(2,128)} copy(f32[1,64,2,256]{3,2,1,0:T(2,128)} %get-tuple-element.8) | data formatting | bytes 262144
  53.3 0.0 copy-done
  53.3 0.6 %copy.16 = f32[4,16,176]{2,1,0:T(8,128)} copy(f32[4,16,176]{2,1,0:T(8,128)S(1)} %bitcast.3) | data formatting | bytes 90112
Async XLA Ops:
  51.7 1.6 %copy-start = (f32[64,176]{1,0:T(8,128)S(1)}, f32[64,176]{1,0:T(8,128)}, u32[]{:S(2)}) copy-start(f32[64,176]{1,0:T(8,128)} %get-tuple-element.5) | copy-start | bytes 135172

commit v9 on v8

--- a/solution.py
+++ b/solution.py
@@ -281,7 +281,7 @@
     send_all(*beam_args[1], 1, STN // 2)
 
     pl.semaphore_wait(column_sem, 1)
-    send_all(*beam_args[0], STN // 2, STN)
+    send_all(*beam_args[0], STN // 2, 48)
 
     for i in range(3, 11):
         load(i).wait()
@@ -404,8 +404,6 @@
         power = fields[:64] * fields[:64] + fields[64:] * fields[64:]
         power_ref[:, first_frame : first_frame + frames] = power[:, :frames] + power[:, frames : 2 * frames]
 
-    beam_power(0)
-
     def hand_over(k):
         other = lax.rem(grp + k, GRP)
         return pltpu.make_async_remote_copy(
@@ -460,10 +458,12 @@
         send_spec.at[1, pl.ds(0, LATE - 1)], recv_spec.at[1, pl.ds(0, LATE - 1)], spec_send_sem.at[1]
     ).wait()
     send_all(*beam_args[1], STN // 2, STN)
+    send_all(*beam_args[0], 48, STN)
     wait_all(*spec_args[1])
     correlate(recv_spec.at[1], pick, 2, False, False, True)
 
     beam_power(1)
+    beam_power(0)
 
     total = part_own[0]
     for k in range(1, GRP):

time: 54 us -> 53.6 us (level)
  no operation moved by 1% of the time
where the time goes in v9:
time: 53.6 us; the launch traced here: 53.5 us
  Pallas kernels  50.6 us (94%)
  local copies, waits for them, and re-layouts  2.23 us (4%)
  between operations  0.65 us (1%)
    pallas_call x1, Pallas kernels, on_device(): pl.pallas_call(kernel, out_shape=(jax.ShapeDtypeStruct((1, 64, 2, 256), F...  50.6 us
    unnamed x4, local copies, waits for them, and re-layouts  2.23 us

profile of v9, /device:TPU:1, one launch (start us, length us, event | category | flops | bytes accessed | tf_op | source)
XLA Modules:
  0.0 53.5 jit_solution(13439495399583712821)
XLA Ops:
  0.6 50.6 %shard_map.122 = (f32[1,64,2,256]{3,2,1,0:T(2,128)}, f32[64,176]{1,0:T(8,128)}) custom-call(bf16[4,2,45056]{2,1,0:T(2,128)(2,1)} %bitcast.2, f32[12,4096]{1,0:T(8,128)} %corr_taps_hbm.1, f32[12,256]{1,0:T(8,128)} %beam_taps_hbm.1, f32[64,256]{1,0:T(8,128)} %angles_hbm.1, s32[16,128]{1,0:T(8,128)} %index_hbm.1, bf16[128,128]{1,0:T(8,128)(2,1)} %constant.12.clone.first_hbm, ...), custom_call_target="tpu_custom_call" | custom-call | tf_op jit(solution)/shard_map/pallas_call | solution.py:497
  51.3 0.0 copy-start
  51.3 1.6 %copy.15 = f32[1,64,2,256]{3,2,1,0:T(2,128)} copy(f32[1,64,2,256]{3,2,1,0:T(2,128)} %get-tuple-element.8) | data formatting | bytes 262144
  52.9 0.0 copy-done
  52.9 0.6 %copy.16 = f32[4,16,176]{2,1,0:T(8,128)} copy(f32[4,16,176]{2,1,0:T(8,128)S(1)} %bitcast.3) | data formatting | bytes 90112
Async XLA Ops:
  51.3 1.6 %copy-start = (f32[64,176]{1,0:T(8,128)S(1)}, f32[64,176]{1,0:T(8,128)}, u32[]{:S(2)}) copy-start(f32[64,176]{1,0:T(8,128)} %get-tuple-element.5) | copy-start | bytes 135172
